TPU v7x, 512 devices: a whole 4x4x16 slice. The times are simulated.
512 devices in a mesh: seq: 32 (over x, y, core), head: 16 (over z).
Axes of the slice: x: 4, y: 4, z: 16, core: 2. Of those that a mesh axis runs over, the one named last changes fastest.
Arguments:
- queries: bfloat16 [16384, 8192], P('seq', 'head'), may hold values from -6 to 6
- keys: bfloat16 [16384, 8192], P('seq', 'head'), may hold values from -6 to 6
- values: bfloat16 [16384, 8192], P('seq', 'head'), may hold values from -6 to 6
- gain: bfloat16 [8192], P('head'), may hold values from 0.25 to 1.75
- d_out: bfloat16 [16384, 8192], P('seq', 'head'), may hold values from -6 to 6
Outputs:
- normed: bfloat16 [16384, 8192], P('seq', 'head')
- d_queries: bfloat16 [16384, 8192], P('seq', 'head')
- d_keys: bfloat16 [16384, 8192], P('seq', 'head')
- d_values: bfloat16 [16384, 8192], P('seq', 'head')
All inputs are finite; a program needn't handle non-finite values.
Results may differ from a plain program's by a relative error of at most 0.0051.
Values sent between devices are 32-bit elements; how exact they have to be, the bound alone decides.
A program may use at most 64 MiB of HBM per device.

v0:
```python
import jax
import jax.numpy as jnp
from jax import lax
from jax.sharding import PartitionSpec as P

DK = 128


def narrow_product(form, left, right):
    return jnp.einsum(form, left, right, preferred_element_type=jnp.float32)


def state_product(form, left, right):
    return jnp.einsum(form, left.astype(jnp.float32), right, precision=lax.Precision.HIGHEST)


def shards(queries, keys, values, gain, d_out):
    rows = queries.shape[0]
    heads_here = queries.shape[1] // DK
    features = heads_here * DK * lax.axis_size("head")
    qb = queries.reshape(rows, heads_here, DK)
    kb = keys.reshape(rows, heads_here, DK)
    vb = values.reshape(rows, heads_here, DK)
    steps = jnp.arange(rows)
    causal = steps[:, None] >= steps[None, :]
    scores = jnp.where(causal, narrow_product("thd,shd->hts", qb, kb), 0.0).astype(jnp.bfloat16)
    own_state = narrow_product("shd,she->hde", kb, vb)
    position = lax.axis_index("seq")
    piece = lax.all_gather(own_state[None], "seq", axis=0, tiled=True)
    index = jnp.arange(piece.shape[0])
    weight = (index < position).astype(jnp.float32)
    prev = jnp.einsum("r,rhde->hde", weight, piece, precision=lax.Precision.HIGHEST)
    attn = narrow_product("hts,she->the", scores, vb) + state_product("thd,hde->the", qb, prev)
    flat = attn.reshape(rows, heads_here * DK)
    squares = lax.psum(jnp.sum(flat * flat, axis=1), "head")
    rms = jnp.sqrt(squares / features + 1e-05)
    gainf = gain.astype(jnp.float32)
    normed = (flat / rms[:, None] * gainf).astype(jnp.bfloat16)
    grad = d_out.astype(jnp.float32) * gainf
    inner = lax.psum(jnp.sum(grad * flat, axis=1), "head") / features
    d_attn = (grad - flat * (inner / (rms * rms))[:, None]) / rms[:, None]
    delta = d_attn.astype(jnp.bfloat16).reshape(rows, heads_here, DK)
    own_grad = narrow_product("thd,the->hde", qb, delta)
    piece = lax.all_gather(own_grad[None], "seq", axis=0, tiled=True)
    index = jnp.arange(piece.shape[0])
    weight = (index > position).astype(jnp.float32)
    later = jnp.einsum("r,rhde->hde", weight, piece, precision=lax.Precision.HIGHEST)
    d_scores = jnp.where(causal, narrow_product("the,she->hts", delta, vb), 0.0).astype(
        jnp.bfloat16
    )
    dq = narrow_product("hts,shd->thd", d_scores, kb) + state_product("the,hde->thd", delta, prev)
    dk = narrow_product("hts,thd->shd", d_scores, qb) + state_product("she,hde->shd", vb, later)
    dv = narrow_product("hts,the->she", scores, delta) + state_product("shd,hde->she", kb, later)
    shape = (rows, heads_here * DK)
    return (
        normed,
        dq.reshape(shape).astype(jnp.bfloat16),
        dk.reshape(shape).astype(jnp.bfloat16),
        dv.reshape(shape).astype(jnp.bfloat16),
    )


def solution(mesh):
    in_specs = (P("seq", "head"), P("seq", "head"), P("seq", "head"), P("head"), P("seq", "head"))
    out_specs = (P("seq", "head"), P("seq", "head"), P("seq", "head"), P("seq", "head"))
    return jax.shard_map(shards, mesh=mesh, in_specs=in_specs, out_specs=out_specs, check_vma=False)
```

profile of v0, /device:TPU:1, one launch (start us, length us, event | category | flops | bytes accessed | tf_op | source)
XLA Modules:
  0.0 220.8 jit_solution(4514371998161148791)
XLA Ops:
  7.2 0.0 copy-start
  7.2 0.0 copy-start.6
  7.2 0.0 all-gather.5.cloned.1.call-start
  7.2 1.3 copy.116
  8.6 0.0 copy-start.5
  8.6 2.2 %fusion.13 = f32[4,128,128]{2,1,0:T(8,128)} fusion(bf16[512,4,128]{0,2,1:T(8,128)(2,1)S(1)} %bitcast.129, bf16[512,512]{1,0:T(8,128)(2,1)} %param.7), kind=kOutput, calls=%fused_computation.29 | convolution fusion | flops 67108864 | bytes 1310720 | tf_op jit(solution)/shard_map/shd,she->hde/dot_general | solution.py:10
  10.8 0.0 all-gather.5.cloned.1.call-update
  10.8 0.0 all-gather.7.cloned.1.call-start
  10.9 0.7 convert_element_type.46
  11.6 0.1 iota_compare_fusion
  11.7 0.0 copy-done
  11.7 0.0 copy-start.10
  11.7 1.9 select_convert_fusion.1
  13.6 0.0 copy-start.1
  13.6 1.4 copy-done.1
  14.9 0.0 copy-done.6
  14.9 0.8 convolution_bitcast_fusion.2
  15.8 0.0 copy-done.5
  15.8 69.9 %all-gather.5.cloned.1.call-done = f32[128,128,128]{2,1,0:T(8,128)} async-done(((f32[4,128,128]{2,1,0:T(8,128)}), f32[128,128,128]{2,1,0:T(8,128)}) %all-gather.5.cloned.1.call-update) | async-done | bytes 8388624 | tf_op jit(solution)/shard_map/all_gather | solution.py:29
  85.7 10.4 %fusion.2 = f32[1,4,128,128]{3,0,2,1:T(1,128)S(1)} fusion(f32[32,4,128,128]{3,2,1,0:T(8,128)} %bitcast.123, s32[]{:T(128)S(6)} %axis_index.15), kind=kOutput, calls=%fused_computation.2 | convolution fusion | flops 25165856 | bytes 8650756 | tf_op jit(solution)/shard_map/r,rhde->hde/dot_general | solution.py:32
  96.1 0.0 copy-done.10
  96.1 1.6 multiply_reduce_fusion.1
  97.8 1.6 copy.40
  99.3 0.0 copy-start.11
  99.3 1.3 multiply_reduce_fusion
  100.6 24.9 %all-reduce = (f32[512]{0:T(512)S(1)}, f32[512]{0:T(512)S(1)}) all-reduce(f32[512]{0:T(512)S(1)} %get-tuple-element.18, f32[512]{0:T(512)S(1)} %multiply_reduce_fusion), channel_id=1, replica_groups=mesh['seq'=32,'head'=16] {'head'}, use_global_device_ids=true, to_apply=%region_1.2 | all-reduce | flops 1024 | bytes 8192 | tf_op jit(solution)/shard_map/psum | solution.py:35
  125.5 2.2 divide_convert_fusion
  127.7 0.2 copy.68
  127.9 0.3 convolution_bitcast_fusion.6
  128.2 0.8 copy.50
  129.1 0.0 all-gather.7.cloned.1.call-update
  129.1 0.0 copy-done.11
  129.1 0.8 select_convert_fusion
  130.0 0.0 copy-start.3
  130.0 1.3 copy-done.3
  131.3 2.0 convolution_bitcast_fusion.1
  133.3 1.4 fusion.7
  134.7 2.0 copy.55
  136.7 0.0 copy-done.2
  136.7 1.5 fusion.39
  138.3 0.4 copy-done.4
  138.7 0.5 convolution_bitcast_fusion
  139.2 60.9 %all-gather.7.cloned.1.call-done = f32[128,128,128]{2,1,0:T(8,128)} async-done(((f32[4,128,128]{2,1,0:T(8,128)}), f32[128,128,128]{2,1,0:T(8,128)}) %all-gather.7.cloned.1.call-update) | async-done | bytes 8388624 | tf_op jit(solution)/shard_map/all_gather | solution.py:44
  200.1 10.6 %fusion = f32[1,4,128,128]{3,0,2,1:T(1,128)S(1)} fusion(f32[32,4,128,128]{3,2,1,0:T(8,128)} %bitcast.124, s32[]{:T(128)S(6)} %axis_index.15), kind=kOutput, calls=%fused_computation | convolution fusion | flops 25165856 | bytes 8650756 | tf_op jit(solution)/shard_map/r,rhde->hde/dot_general | solution.py:47
  210.7 0.7 fusion.9
  211.4 1.0 copy.57
  212.4 0.6 fusion.8
  213.0 1.0 copy.56
  (9 shorter events, 0.0 us)
Async XLA Ops:
  7.2 4.5 %copy-start = (bf16[512,512]{1,0:T(8,128)(2,1)S(1)}, bf16[512,512]{1,0:T(8,128)(2,1)}, u32[]{:S(2)}) copy-start(bf16[512,512]{1,0:T(8,128)(2,1)} %param.5) | copy-start | bytes 1572868
  7.2 7.8 %copy-start.6 = (bf16[512,512]{1,0:T(8,128)(2,1)S(1)}, bf16[512,512]{1,0:T(8,128)(2,1)}, u32[]{:S(2)}) copy-start(bf16[512,512]{1,0:T(8,128)(2,1)} %param.7) | copy-start | bytes 1572868
  7.2 78.5 %all-gather.5.cloned.1.call-start = ((), (), s32[]{:S(2)}) async-start(), calls=%async_computation | async-start | bytes 8650752 | tf_op jit(solution)/shard_map/all_gather | solution.py:29
  8.6 7.2 %copy-start.5 = (bf16[512,512]{0,1:T(8,128)(2,1)}, bf16[512,512]{0,1:T(8,128)(2,1)S(1)}, u32[]{:S(2)}) copy-start(bf16[512,512]{0,1:T(8,128)(2,1)S(1)} %copy.116) | copy-start | bytes 1572868
  10.8 189.3 %all-gather.7.cloned.1.call-start = ((), (), s32[]{:S(2)}) async-start(), calls=%async_computation.1 | async-start | bytes 8650752 | tf_op jit(solution)/shard_map/all_gather | solution.py:44
  11.7 84.5 %copy-start.10 = (pred[512,512]{1,0:T(8,128)(4,1)}, pred[512,512]{1,0:T(8,128)(4,1)S(1)}, u32[]{:S(2)}) copy-start(pred[512,512]{1,0:T(8,128)(4,1)S(1)} %iota_compare_fusion) | copy-start | bytes 786436
  13.6 1.4 copy-start.1
  99.3 29.8 %copy-start.11 = (pred[512,512]{1,0:T(8,128)(4,1)S(1)}, pred[512,512]{1,0:T(8,128)(4,1)}, u32[]{:S(2)}) copy-start(pred[512,512]{1,0:T(8,128)(4,1)} %copy-done.10) | copy-start | bytes 786436
  130.0 1.3 copy-start.3
  131.3 5.4 %copy-start.2 = (bf16[4,512,512]{2,1,0:T(8,128)(2,1)S(1)}, bf16[4,512,512]{2,1,0:T(8,128)(2,1)}, u32[]{:S(2)}) copy-start(bf16[4,512,512]{2,1,0:T(8,128)(2,1)} %copy-done.1) | copy-start | bytes 6291460
  136.7 2.0 copy-start.4
  200.1 10.6 %copy-start.8 = (f32[4,128,512]{2,1,0:T(8,128)S(1)}, f32[4,128,512]{2,1,0:T(8,128)}, u32[]{:S(2)}) copy-start(f32[4,128,512]{2,1,0:T(8,128)} %fusion.39) | copy-start | bytes 3145732
  200.1 10.6 %copy-start.9 = (bf16[512,512]{1,0:T(8,128)(2,1)S(1)}, bf16[512,512]{1,0:T(8,128)(2,1)}, u32[]{:S(2)}) copy-start(bf16[512,512]{1,0:T(8,128)(2,1)} %param.6) | copy-start | bytes 1572868
  200.1 12.3 %copy-start.7 = (bf16[512,512]{1,0:T(8,128)(2,1)S(1)}, bf16[512,512]{1,0:T(8,128)(2,1)}, u32[]{:S(2)}) copy-start(bf16[512,512]{1,0:T(8,128)(2,1)} %param.7) | copy-start | bytes 1572868
Sparse Core Ops, SparseCore 0:
  11.7 73.9 all-gather.4
  129.2 70.8 all-gather.6
where the time goes:
time: 221 us
  waiting for transfers between devices  131 us (59%)
  matrix products  35.3 us (16%)
  blocking collectives  24.9 us (11%)
  between operations  14.2 us (6%)
  local copies, waits for them, and re-layouts  11.2 us (5%)
  other arithmetic  4.24 us (2%)
    all_gather x1, waiting for transfers between devices, shards(): piece = lax.all_gather(own_state[None], 'seq', axis=0, tiled=True)  69.9 us
    all_gather x1, waiting for transfers between devices, shards(): piece = lax.all_gather(own_grad[None], 'seq', axis=0, tiled=True)  60.9 us
    psum x1, blocking collectives, shards(): squares = lax.psum(jnp.sum(flat * flat, axis=1), 'head')  24.9 us
    dot_general x2, matrix products, shards(): jnp.einsum('r,rhde->hde', weight, piece, precision=lax.Precision.HIGHEST)  21 us
    dot_general x8, matrix products, narrow_product(): return jnp.einsum(form, left, right, preferred_element_type=jnp.float32)  10.1 us
    unnamed x27, local copies, waits for them, and re-layouts  7.24 us
  transfers between devices with their start and end apart: 2, of which 2 were waited for; matrix products, arithmetic and copies ran while one was open for 5% of the time, Pallas kernels for 0%

commit v1 on v0

v1 whole, which is shorter than its diff:
```python
import functools

import jax
import jax.numpy as jnp
from jax import lax
from jax.experimental import pallas as pl
from jax.experimental.pallas import tpu as pltpu
from jax.sharding import PartitionSpec as P

DK = 128
ROWS = 512
HEADS_HERE = 4
FEATURES = 8192
SIDE = 4
DEPTH = 16
MESH = pl.DeviceIdType.MESH
F32 = jnp.float32
BF16 = jnp.bfloat16

NN = (((1,), (0,)), ((), ()))
NT = (((1,), (1,)), ((), ()))
TN = (((0,), (0,)), ((), ()))


def dot(left, right, dims):
    return lax.dot_general(left, right, dims, preferred_element_type=F32)


def head(h):
    return pl.ds(h * DK, DK)


def halves(state, axis):
    high = state.astype(BF16)
    low = (state - high.astype(F32)).astype(BF16)
    return jnp.concatenate([high, low], axis=axis)


def body(
    q_hbm, k_hbm, v_hbm, gain_ref, d_hbm,
    normed_hbm, dq_hbm, dk_hbm, dv_hbm,
    q, k, v, d, normed, dq, dk, dv,
    qt, scores_t, attn, g, e, dk_part, dv_part,
    own, sib, chip, recv1, row, cols, recv2, pref,
    zsend, zrecv,
    load_sem, store_sem, send_sem, recv_sem, zsend_sem, zrecv_sem,
):
    s = lax.axis_index("seq")
    z = lax.axis_index("head")
    x, y, c = s // 8, (s // 2) % SIDE, s % 2
    sibling = (s + 1 - 2 * c, z)

    def along_y(step):
        return (x * 8 + ((y + step) % SIDE) * 2 + c, z)

    def along_x(step):
        return (((x + step) % SIDE) * 8 + y * 2 + c, z)

    def along_z(step):
        return (s, (z + step) % DEPTH)

    loads = [
        pltpu.make_async_copy(src, dst, load_sem.at[i])
        for i, (src, dst) in enumerate(((k_hbm, k), (v_hbm, v), (q_hbm, q), (d_hbm, d)))
    ]
    for load in loads:
        load.start()

    barrier = pltpu.get_barrier_semaphore()
    partners = [sibling]
    partners += [along_y(i) for i in range(1, SIDE)] + [along_x(i) for i in range(1, SIDE)]
    partners += [along_z(i) for i in range(1, DEPTH)]
    for partner in partners:
        pl.semaphore_signal(barrier, inc=1, device_id=partner, device_id_type=MESH)

    def message(way, number):
        here, there = pl.ds(256 * c, 256), pl.ds(256 * (1 - c), 256)
        if number == 0:
            src, dst, device = own.at[way, there], sib.at[way, 0], sibling
        elif number == 1:
            src, dst, device = own.at[way, here], sib.at[way, 1], sibling
        elif number == 2:
            src, dst, device = pref.at[way, here], pref.at[way, here], sibling
        elif number < 6:
            step = number - 2
            src, dst, device = chip.at[way, pl.ds(0, 128)], recv1.at[way, 0, step - 1], along_y(step)
        elif number < 9:
            step = number - 5
            src, dst, device = chip.at[way, pl.ds(128, 128)], recv1.at[way, 1, step - 1], along_x(step)
        elif number < 12:
            step = number - 8
            src, dst, device = row.at[way], recv2.at[way, 0, step - 1], along_x(step)
        else:
            step = number - 11
            wrapped = (y + step) // SIDE
            pick = 1 - wrapped if way == 0 else wrapped
            src, dst, device = cols.at[way, pick], recv2.at[way, 1, step - 1], along_y(step)
        return pltpu.make_async_remote_copy(
            src_ref=src, dst_ref=dst, send_sem=send_sem.at[way, number], recv_sem=recv_sem.at[way, number],
            device_id=device, device_id_type=MESH,
        )

    def zmessage(step):
        return pltpu.make_async_remote_copy(
            src_ref=zsend, dst_ref=zrecv.at[step - 1], send_sem=zsend_sem.at[step - 1],
            recv_sem=zrecv_sem.at[step - 1], device_id=along_z(step), device_id_type=MESH,
        )

    def counts(way, step, place):
        return step <= place if way == 0 else step > place

    def start_pair(way):
        message(way, 0).start()
        message(way, 1).start()

    def start_first(way):
        message(way, 0).wait_recv()
        chip[way] = own[way, pl.ds(256 * c, 256)] + sib[way, 0]
        for number in (4, 7, 3, 5, 6, 8):
            message(way, number).start()

    def start_second(way):
        for number in range(3, 9):
            message(way, number).wait_recv()
        mine = chip[way, pl.ds(0, 128)]
        total, before = mine, jnp.zeros_like(mine)
        for step in range(1, SIDE):
            block = recv1[way, 0, step - 1]
            total = total + block
            before = before + jnp.where(counts(way, step, y), block, 0.0)
        row[way] = total
        pref[way, pl.ds(256 * c, 128)] = before
        column = jnp.zeros_like(mine)
        for step in range(1, SIDE):
            column = column + jnp.where(counts(way, step, x), recv1[way, 1, step - 1], 0.0)
        cols[way, 0] = column
        cols[way, 1] = column + chip[way, pl.ds(128, 128)]
        for number in (10, 13, 9, 11, 12, 14):
            message(way, number).start()

    def start_third(way):
        for number in range(9, 15):
            message(way, number).wait_recv()
        first = pref[way, pl.ds(256 * c, 128)]
        second = cols[way, 0]
        for step in range(1, SIDE):
            first = first + jnp.where(counts(way, step, x), recv2[way, 0, step - 1], 0.0)
            second = second + recv2[way, 1, step - 1]
        pref[way, pl.ds(256 * c, 128)] = first
        pref[way, pl.ds(256 * c + 128, 128)] = second
        message(way, 2).start()
        message(way, 1).wait_recv()

    def state(way, h):
        half = h // 2
        other = (half + c) % 2
        add = c == 1 if way == 0 else c == 0
        block = sib[way, other, pl.ds((h % 2) * DK, DK)]
        return pref[way, pl.ds(h * DK, DK)] + jnp.where(add, block, 0.0)

    steps0 = lax.broadcasted_iota(jnp.int32, (DK, DK), 0)
    steps1 = lax.broadcasted_iota(jnp.int32, (DK, DK), 1)

    def causal(block, lower):
        keep = steps0 >= steps1 if lower else steps0 <= steps1
        if block.shape[1] == DK:
            return jnp.where(keep, block, 0.0).astype(BF16)
        if lower:
            cut = block.shape[1] - DK
            return jnp.concatenate(
                [block[:, :cut].astype(BF16), jnp.where(keep, block[:, cut:], 0.0).astype(BF16)], axis=1
            )
        return jnp.concatenate(
            [jnp.where(keep, block[:, :DK], 0.0).astype(BF16), block[:, DK:].astype(BF16)], axis=1
        )

    loads[0].wait()
    loads[1].wait()
    for h in range(HEADS_HERE):
        own[0, head(h)] = dot(k[:, head(h)], v[:, head(h)], TN)
    pl.semaphore_wait(barrier, len(partners))
    start_pair(0)
    loads[2].wait()
    loads[3].wait()

    start_first(0)

    def inner(h, carry):
        at = pl.ds(pl.multiple_of(h * DK, DK), DK)
        for r in range(4):
            strip = causal(dot(q[pl.ds(r * DK, DK), at], k[pl.ds(0, (r + 1) * DK), at], NT), True)
            attn[pl.ds(r * DK, DK), at] = dot(strip, v[pl.ds(0, (r + 1) * DK), at], NN)
        return carry

    lax.fori_loop(0, HEADS_HERE, inner, 0)
    start_second(0)

    def prepare(h, carry):
        at = pl.ds(pl.multiple_of(h * DK, DK), DK)
        qt[at, :] = q[:, at].astype(F32).T.astype(BF16)
        g[:, at] = d[:, at].astype(F32) * gain_ref[:, at]
        for r in range(4):
            rest = ROWS - r * DK
            strip = dot(k[pl.ds(r * DK, DK), at], q[pl.ds(r * DK, rest), at], NT)
            scores_t[h, pl.ds(r * DK, DK), pl.ds(r * DK, rest)] = causal(strip, False)
        return carry

    lax.fori_loop(0, HEADS_HERE, prepare, 0)
    start_third(0)
    message(0, 2).wait_recv()

    squares = jnp.zeros((ROWS, DK), F32)
    products = jnp.zeros((ROWS, DK), F32)
    for h in range(HEADS_HERE):
        qh = q[:, head(h)]
        total = attn[:, head(h)] + dot(jnp.concatenate([qh, qh], axis=1), halves(state(0, h), 0), NN)
        attn[:, head(h)] = total
        squares = squares + total * total
        products = products + total * g[:, head(h)]

    ones = jnp.ones((8, 3 * DK), BF16)

    def row_sums(array):
        high = array.astype(BF16)
        rest = array - high.astype(F32)
        middle = rest.astype(BF16)
        low = (rest - middle.astype(F32)).astype(BF16)
        return dot(ones, jnp.concatenate([high, middle, low], axis=1), NT)

    for i, array in enumerate((squares, products)):
        sums = row_sums(array)
        for j in range(4):
            zsend[pl.ds(4 * i + j, 1), :] = sums[0:1, j * DK : (j + 1) * DK]
    for step in (8, 7, 9, 6, 10, 5, 11, 4, 12, 3, 13, 2, 14, 1, 15):
        zmessage(step).start()

    totals = zsend[...]
    for step in range(1, DEPTH):
        zmessage(step).wait_recv()
    for step in range(1, DEPTH):
        totals = totals + zrecv[step - 1]
    means = totals / FEATURES
    rms = jnp.sqrt(means[0:4] + 1e-05)
    inverse = 1.0 / rms
    weight = means[4:8] * inverse * inverse
    columns = jnp.concatenate([inverse, weight], axis=0).T
    for j in range(4):
        at = pl.ds(j * DK, DK)
        delta = (g[at, :] - attn[at, :] * columns[:, 4 + j : 5 + j]) * columns[:, j : j + 1]
        e[at, :] = delta.astype(BF16)

    for h in range(HEADS_HERE):
        own[1, head(h)] = dot(qt[head(h), :], e[:, head(h)], NN)
    start_pair(1)
    for j in range(4):
        at = pl.ds(j * DK, DK)
        normed[at, :] = (attn[at, :] * columns[:, j : j + 1] * gain_ref[...]).astype(BF16)
    start_first(1)
    stores = [
        pltpu.make_async_copy(src, dst, store_sem.at[i])
        for i, (src, dst) in enumerate(((normed, normed_hbm), (dq, dq_hbm), (dk, dk_hbm), (dv, dv_hbm)))
    ]
    stores[0].start()

    def outer(h, carry):
        at = pl.ds(pl.multiple_of(h * DK, DK), DK)
        for r in range(4):
            low, rest = pl.ds(r * DK, DK), ROWS - r * DK
            strip = causal(dot(v[low, at], e[pl.ds(r * DK, rest), at], NT), False)
            dk_part[low, at] = dot(strip, q[pl.ds(r * DK, rest), at], NN)
            dv_part[low, at] = dot(scores_t[h, low, pl.ds(r * DK, rest)], e[pl.ds(r * DK, rest), at], NN)
        return carry

    lax.fori_loop(0, HEADS_HERE, outer, 0)
    start_second(1)

    for h in range(HEADS_HERE):
        back = halves(state(0, h), 1)
        for r in range(4):
            low = pl.ds(r * DK, DK)
            eh = e[low, head(h)]
            strip = causal(dot(eh, v[pl.ds(0, (r + 1) * DK), head(h)], NT), True)
            total = dot(strip, k[pl.ds(0, (r + 1) * DK), head(h)], NN)
            dq[low, head(h)] = (total + dot(jnp.concatenate([eh, eh], axis=1), back, NT)).astype(BF16)
    stores[1].start()
    start_third(1)
    message(1, 2).wait_recv()

    for h in range(HEADS_HERE):
        later = state(1, h)
        vh, kh = v[:, head(h)], k[:, head(h)]
        total = dk_part[:, head(h)] + dot(jnp.concatenate([vh, vh], axis=1), halves(later, 1), NT)
        dk[:, head(h)] = total.astype(BF16)
        total = dv_part[:, head(h)] + dot(jnp.concatenate([kh, kh], axis=1), halves(later, 0), NN)
        dv[:, head(h)] = total.astype(BF16)
    stores[2].start()
    stores[3].start()
    for way in range(2):
        for number in range(15):
            message(way, number).wait_send()
    for step in range(1, DEPTH):
        zmessage(step).wait_send()
    for store in stores:
        store.wait()


def shards(queries, keys, values, gain, d_out):
    whole = jax.ShapeDtypeStruct((ROWS, HEADS_HERE * DK), BF16)
    block = pltpu.VMEM((ROWS, HEADS_HERE * DK), BF16)
    wide = pltpu.VMEM((ROWS, HEADS_HERE * DK), F32)
    square = (DK, DK)
    anywhere = pl.BlockSpec(memory_space=pl.ANY)
    return pl.pallas_call(
        body,
        out_shape=[whole] * 4,
        in_specs=[anywhere, anywhere, anywhere, pl.BlockSpec(memory_space=pltpu.VMEM), anywhere],
        out_specs=[anywhere] * 4,
        scratch_shapes=[block] * 8
        + [
            pltpu.VMEM((HEADS_HERE * DK, ROWS), BF16),
            pltpu.VMEM((HEADS_HERE, ROWS, ROWS), BF16),
            wide, wide, block, wide, wide,
            pltpu.VMEM((2, 512, DK), F32),
            pltpu.VMEM((2, 2, 256, DK), F32),
            pltpu.VMEM((2, 256, DK), F32),
            pltpu.VMEM((2, 2, 3) + square, F32),
            pltpu.VMEM((2,) + square, F32),
            pltpu.VMEM((2, 2) + square, F32),
            pltpu.VMEM((2, 2, 3) + square, F32),
            pltpu.VMEM((2, 512, DK), F32),
            pltpu.VMEM((8, DK), F32),
            pltpu.VMEM((DEPTH - 1, 8, DK), F32),
            pltpu.SemaphoreType.DMA((4,)),
            pltpu.SemaphoreType.DMA((4,)),
            pltpu.SemaphoreType.DMA((2, 15)),
            pltpu.SemaphoreType.DMA((2, 15)),
            pltpu.SemaphoreType.DMA((DEPTH - 1,)),
            pltpu.SemaphoreType.DMA((DEPTH - 1,)),
        ],
        compiler_params=pltpu.CompilerParams(
            collective_id=0, has_side_effects=True, vmem_limit_bytes=32 * 1024 * 1024
        ),
        name="attention",
    )(queries, keys, values, gain.astype(F32).reshape(1, HEADS_HERE * DK), d_out)


def solution(mesh):
    in_specs = (P("seq", "head"), P("seq", "head"), P("seq", "head"), P("head"), P("seq", "head"))
    out_specs = (P("seq", "head"), P("seq", "head"), P("seq", "head"), P("seq", "head"))
    return jax.shard_map(shards, mesh=mesh, in_specs=in_specs, out_specs=out_specs, check_vma=False)
```

time: 221 us -> 61.8 us (0.28)
  waiting for transfers between devices: 131 us -> 0 us
  Pallas kernels: 0 us -> 52.9 us
  matrix products: 35.3 us -> 0 us
  blocking collectives: 24.9 us -> 0 us
  between operations: 14.2 us -> 0.64 us
  local copies, waits for them, and re-layouts: 11.2 us -> 7.34 us
  other arithmetic: 4.24 us -> 0.68 us
    all_gather x2 -> x0, waiting for transfers between devices: 131 us -> none  [the longest x1 69.9 us: shards(): piece = lax.all_gather(own_state[None], 'seq', axis=0, tiled=True)]
    pallas_call x0 -> x1, Pallas kernels: none -> 52.9 us  [shards(): pl.pallas_call(body, out_shape=[whole] * 4, in_specs=[anywhere, anywhere,...]
    dot_general x14 -> x0, matrix products: 35.3 us -> none  [the longest x2 21 us: shards(): jnp.einsum('r,rhde->hde', weight, piece, precision=lax.Precision.HIGHEST)]
    psum x1 -> x0, blocking collectives: 24.9 us -> none  [shards(): squares = lax.psum(jnp.sum(flat * flat, axis=1), 'head')]
    reshape x3 -> x0, local copies, waits for them, and re-layouts: 3.1 us -> none  [the longest x1 1.55 us: shards(): flat = attn.reshape(rows, heads_here * DK)]
    convert_element_type x2 -> x0, other arithmetic: 2.85 us -> none  [the longest x1 2.17 us: shards(): delta = d_attn.astype(jnp.bfloat16).reshape(rows, heads_here, DK)]
    unnamed x27 -> x12, local copies, waits for them, and re-layouts: 7.24 us -> 7.34 us
  transfers between devices with their start and end apart: 2 -> 0, of which waited for: 2 -> 0; matrix products, arithmetic and copies ran while one was open for 5% -> 0% of each run, Pallas kernels for 0% -> 0%
where the time goes in v1:
time: 61.8 us; the launch traced here: 61.5 us
  Pallas kernels  52.9 us (86%)
  local copies, waits for them, and re-layouts  7.34 us (12%)
  other arithmetic  0.68 us (1%)
  between operations  0.64 us (1%)
    pallas_call x1, Pallas kernels, shards(): pl.pallas_call(body, out_shape=[whole] * 4, in_specs=[anywhere, anywhere,...  52.9 us
    unnamed x12, local copies, waits for them, and re-layouts  7.34 us

profile of v1, /device:TPU:1, one launch (start us, length us, event | category | flops | bytes accessed | tf_op | source)
XLA Modules:
  0.0 61.5 jit_solution(5743663304239254671)
XLA Ops:
  0.6 0.7 %reshape.15 = f32[512]{0:T(512)S(1)} convert(bf16[512]{0:T(512)(128)(2,1)} %param.8) | non-fusion elementwise | flops 512 | bytes 3072 | tf_op jit(solution)/shard_map/reshape | solution.py:344
  1.3 0.0 copy-start
  1.3 1.0 %copy-done = bf16[512,512]{1,0:T(8,128)(2,1)S(1)} copy-done((bf16[512,512]{1,0:T(8,128)(2,1)S(1)}, bf16[512,512]{1,0:T(8,128)(2,1)}, u32[]{:S(2)}) %copy-start) | copy-done | bytes 524312
  2.4 0.0 copy-start.1
  2.4 1.0 %copy-done.1 = bf16[512,512]{1,0:T(8,128)(2,1)S(1)} copy-done((bf16[512,512]{1,0:T(8,128)(2,1)S(1)}, bf16[512,512]{1,0:T(8,128)(2,1)}, u32[]{:S(2)}) %copy-start.1) | copy-done | bytes 524312
  3.4 0.0 copy-start.2
  3.4 1.0 %copy-done.2 = bf16[512,512]{1,0:T(8,128)(2,1)S(1)} copy-done((bf16[512,512]{1,0:T(8,128)(2,1)S(1)}, bf16[512,512]{1,0:T(8,128)(2,1)}, u32[]{:S(2)}) %copy-start.2) | copy-done | bytes 524312
  4.4 0.0 copy-start.3
  4.4 1.0 %copy-done.3 = bf16[512,512]{1,0:T(8,128)(2,1)S(1)} copy-done((bf16[512,512]{1,0:T(8,128)(2,1)S(1)}, bf16[512,512]{1,0:T(8,128)(2,1)}, u32[]{:S(2)}) %copy-start.3) | copy-done | bytes 524312
  5.5 52.9 %attention.1 = (bf16[512,512]{1,0:T(8,128)(2,1)S(1)}, bf16[512,512]{1,0:T(8,128)(2,1)S(1)}, bf16[512,512]{1,0:T(8,128)(2,1)S(1)}, bf16[512,512]{1,0:T(8,128)(2,1)S(1)}) custom-call(bf16[512,512]{1,0:T(8,128)(2,1)S(1)} %copy-done, bf16[512,512]{1,0:T(8,128)(2,1)S(1)} %copy-done.1, bf16[512,512]{1,0:T(8,128)(2,1)S(1)} %copy-done.2, f32[1,512]{1,0:T(1,128)S(1)} %bitcast.1, ...), custom_call_target="tpu_custom_call" | custom-call | tf_op jit(solution)/shard_map/attention/pallas_call | solution.py:313
  58.3 0.8 %copy.13 = bf16[512,512]{1,0:T(8,128)(2,1)} copy(bf16[512,512]{1,0:T(8,128)(2,1)S(1)} %get-tuple-element.8) | data formatting | bytes 1048576
  59.1 0.8 %copy.14 = bf16[512,512]{1,0:T(8,128)(2,1)} copy(bf16[512,512]{1,0:T(8,128)(2,1)S(1)} %get-tuple-element.9) | data formatting | bytes 1048576
  59.9 0.8 %copy.15 = bf16[512,512]{1,0:T(8,128)(2,1)} copy(bf16[512,512]{1,0:T(8,128)(2,1)S(1)} %get-tuple-element.10) | data formatting | bytes 1048576
  60.7 0.8 %copy.16 = bf16[512,512]{1,0:T(8,128)(2,1)} copy(bf16[512,512]{1,0:T(8,128)(2,1)S(1)} %get-tuple-element.11) | data formatting | bytes 1048576
Async XLA Ops:
  1.3 1.0 %copy-start = (bf16[512,512]{1,0:T(8,128)(2,1)S(1)}, bf16[512,512]{1,0:T(8,128)(2,1)}, u32[]{:S(2)}) copy-start(bf16[512,512]{1,0:T(8,128)(2,1)} %q_hbm.1) | copy-start | bytes 1572868
  2.4 1.0 %copy-start.1 = (bf16[512,512]{1,0:T(8,128)(2,1)S(1)}, bf16[512,512]{1,0:T(8,128)(2,1)}, u32[]{:S(2)}) copy-start(bf16[512,512]{1,0:T(8,128)(2,1)} %k_hbm.1) | copy-start | bytes 1572868
  3.4 1.0 %copy-start.2 = (bf16[512,512]{1,0:T(8,128)(2,1)S(1)}, bf16[512,512]{1,0:T(8,128)(2,1)}, u32[]{:S(2)}) copy-start(bf16[512,512]{1,0:T(8,128)(2,1)} %v_hbm.1) | copy-start | bytes 1572868
  4.4 1.0 %copy-start.3 = (bf16[512,512]{1,0:T(8,128)(2,1)S(1)}, bf16[512,512]{1,0:T(8,128)(2,1)}, u32[]{:S(2)}) copy-start(bf16[512,512]{1,0:T(8,128)(2,1)} %d_hbm.1) | copy-start | bytes 1572868

commit v2 on v1

v2 whole, which is shorter than its diff:
```python
import functools

import jax
import jax.numpy as jnp
from jax import lax
from jax.experimental import pallas as pl
from jax.experimental.pallas import tpu as pltpu
from jax.sharding import PartitionSpec as P

DK = 128
ROWS = 512
HEADS_HERE = 4
FEATURES = 8192
SIDE = 4
DEPTH = 16
MESH = pl.DeviceIdType.MESH
F32 = jnp.float32
BF16 = jnp.bfloat16

NN = (((1,), (0,)), ((), ()))
NT = (((1,), (1,)), ((), ()))
TN = (((0,), (0,)), ((), ()))


def dot(left, right, dims):
    return lax.dot_general(left, right, dims, preferred_element_type=F32)


def head(h):
    return pl.ds(h * DK, DK)


def halves(state, axis):
    high = state.astype(BF16)
    low = (state - high.astype(F32)).astype(BF16)
    return jnp.concatenate([high, low], axis=axis)


def body(
    q_hbm, k_hbm, v_hbm, gain_hbm, d_hbm,
    normed, dq, dk_part, dv_part, later, k, v,
    q, d, gain,
    qt, scores_t, attn, g, e,
    own, sib, chip, recv1, row, cols, recv2, pref,
    zsend, zrecv,
    load_sem, send_sem, recv_sem, zsend_sem, zrecv_sem, near_sem,
):
    s = lax.axis_index("seq")
    z = lax.axis_index("head")
    x, y, c = s // 8, (s // 2) % SIDE, s % 2
    sibling = (s + 1 - 2 * c, z)

    def along_y(step):
        return (x * 8 + ((y + step) % SIDE) * 2 + c, z)

    def along_x(step):
        return (((x + step) % SIDE) * 8 + y * 2 + c, z)

    def along_z(step):
        return (s, (z + step) % DEPTH)

    loads = [
        pltpu.make_async_copy(src, dst, load_sem.at[i])
        for i, (src, dst) in enumerate(((k_hbm, k), (v_hbm, v), (q_hbm, q), (d_hbm, d), (gain_hbm, gain)))
    ]
    for load in loads:
        load.start()

    barrier = pltpu.get_barrier_semaphore()
    partners = [sibling, along_z(1), along_z(DEPTH - 1)]
    partners += [along_y(i) for i in range(1, SIDE)] + [along_x(i) for i in range(1, SIDE)]
    for partner in partners:
        pl.semaphore_signal(barrier, inc=1, device_id=partner, device_id_type=MESH)

    def tell(turn):
        for step in (2**turn, DEPTH - 2**turn):
            pl.semaphore_signal(near_sem.at[turn], inc=1, device_id=along_z(step), device_id_type=MESH)

    def hear(turn):
        pl.semaphore_wait(near_sem.at[turn], 2)

    def half_head(half, j):
        return pl.ds(pl.multiple_of((2 * half + j) * DK, DK), DK)

    def message(way, number, src, dst, device):
        return pltpu.make_async_remote_copy(
            src_ref=src, dst_ref=dst, send_sem=send_sem.at[way, number], recv_sem=recv_sem.at[way, number],
            device_id=device, device_id_type=MESH,
        )

    def sib_message(way, j):
        if j == 2:
            return message(way, 2, own.at[way, pl.ds(256 * c, 256)], sib.at[way, 1], sibling)
        return message(way, j, own.at[way, half_head(1 - c, j)], sib.at[way, 0, pl.ds(j * DK, DK)], sibling)

    def pref_message(way, j):
        return message(way, 3 + j, pref.at[way, half_head(c, j)], pref.at[way, half_head(c, j)], sibling)

    def plane_message(way, phase, j, a, step):
        number = 5 + ((phase * 2 + j) * 2 + a) * 3 + step - 1
        device = along_y(step) if phase == a else along_x(step)
        if phase == 0:
            src, dst = chip.at[way, j, a], recv1.at[way, j, a, step - 1]
        elif a == 0:
            src, dst = row.at[way, j], recv2.at[way, j, a, step - 1]
        else:
            wrapped = (y + step) // SIDE
            pick = 1 - wrapped if way == 0 else wrapped
            src, dst = cols.at[way, j, pick], recv2.at[way, j, a, step - 1]
        return message(way, number, src, dst, device)

    def zmessage(step):
        return pltpu.make_async_remote_copy(
            src_ref=zsend, dst_ref=zrecv.at[step - 1], send_sem=zsend_sem.at[step - 1],
            recv_sem=zrecv_sem.at[step - 1], device_id=along_z(step), device_id_type=MESH,
        )

    def counts(way, step, place):
        return step <= place if way == 0 else step > place

    def start_first(way):
        for j in range(2):
            sib_message(way, j).wait_recv()
            total = own[way, half_head(c, j)] + sib[way, 0, pl.ds(j * DK, DK)]
            for a in range(2):
                chip[way, j, a] = total[64 * a : 64 * a + 64]
            for step in (2, 1, 3):
                for a in range(2):
                    plane_message(way, 0, j, a, step).start()

    def start_second(way):
        for j in range(2):
            for a in range(2):
                for step in range(1, SIDE):
                    plane_message(way, 0, j, a, step).wait_recv()
                mine = chip[way, j, a]
                if a == 0:
                    total, before = mine, jnp.zeros_like(mine)
                    for step in range(1, SIDE):
                        block = recv1[way, j, a, step - 1]
                        total = total + block
                        before = before + jnp.where(counts(way, step, y), block, 0.0)
                    row[way, j] = total
                    pref[way, pl.ds(256 * c + j * DK, 64)] = before
                else:
                    column = jnp.zeros_like(mine)
                    for step in range(1, SIDE):
                        column = column + jnp.where(counts(way, step, x), recv1[way, j, a, step - 1], 0.0)
                    cols[way, j, 0] = column
                    cols[way, j, 1] = column + mine
                for step in (2, 1, 3):
                    plane_message(way, 1, j, a, step).start()

    def start_third(way):
        for j in range(2):
            for a in range(2):
                for step in range(1, SIDE):
                    plane_message(way, 1, j, a, step).wait_recv()
                at = pl.ds(256 * c + j * DK + 64 * a, 64)
                if a == 0:
                    total = pref[way, at]
                    for step in range(1, SIDE):
                        total = total + jnp.where(counts(way, step, x), recv2[way, j, a, step - 1], 0.0)
                else:
                    total = cols[way, j, 0]
                    for step in range(1, SIDE):
                        total = total + recv2[way, j, a, step - 1]
                pref[way, at] = total
            pref_message(way, j).start()

    def state(way, mine, j):
        add = c == 1 if way == 0 else c == 0
        block = sib[way, 0 if mine else 1, pl.ds(j * DK, DK)]
        return pref[way, half_head(c if mine else 1 - c, j)] + jnp.where(add, block, 0.0)

    steps0 = lax.broadcasted_iota(jnp.int32, (DK, DK), 0)
    steps1 = lax.broadcasted_iota(jnp.int32, (DK, DK), 1)

    def causal(block, lower):
        keep = steps0 >= steps1 if lower else steps0 <= steps1
        if block.shape[1] == DK:
            return jnp.where(keep, block, 0.0).astype(BF16)
        if lower:
            cut = block.shape[1] - DK
            return jnp.concatenate(
                [block[:, :cut].astype(BF16), jnp.where(keep, block[:, cut:], 0.0).astype(BF16)], axis=1
            )
        return jnp.concatenate(
            [jnp.where(keep, block[:, :DK], 0.0).astype(BF16), block[:, DK:].astype(BF16)], axis=1
        )

    loads[0].wait()
    loads[1].wait()
    for j in range(2):
        at = half_head(1 - c, j)
        own[0, at] = dot(k[:, at], v[:, at], TN)
    pl.semaphore_wait(barrier, len(partners))
    tell(0)
    for j in range(2):
        sib_message(0, j).start()
    for j in range(2):
        at = half_head(c, j)
        own[0, at] = dot(k[:, at], v[:, at], TN)
    sib_message(0, 2).start()
    loads[2].wait()
    loads[3].wait()
    loads[4].wait()
    start_first(0)

    def inner(h, carry):
        at = pl.ds(pl.multiple_of(h * DK, DK), DK)
        for r in range(4):
            strip = causal(dot(q[pl.ds(r * DK, DK), at], k[pl.ds(0, (r + 1) * DK), at], NT), True)
            attn[pl.ds(r * DK, DK), at] = dot(strip, v[pl.ds(0, (r + 1) * DK), at], NN)
        return carry

    lax.fori_loop(0, HEADS_HERE, inner, 0)
    hear(0)
    tell(1)
    start_second(0)

    gains = gain[...].astype(F32)

    def prepare(h, carry):
        at = pl.ds(pl.multiple_of(h * DK, DK), DK)
        qt[at, :] = q[:, at].astype(F32).T.astype(BF16)
        for r in range(4):
            rest = ROWS - r * DK
            strip = dot(k[pl.ds(r * DK, DK), at], q[pl.ds(r * DK, rest), at], NT)
            scores_t[h, pl.ds(r * DK, DK), pl.ds(r * DK, rest)] = causal(strip, False)
        return carry

    lax.fori_loop(0, HEADS_HERE, prepare, 0)
    g[...] = d[...].astype(F32) * gains
    hear(1)
    tell(2)
    start_third(0)
    sib_message(0, 2).wait_recv()

    squares = jnp.zeros((ROWS, DK), F32)
    products = jnp.zeros((ROWS, DK), F32)
    for mine in (True, False):
        for j in range(2):
            if not mine:
                pref_message(0, j).wait_recv()
            at = half_head(c if mine else 1 - c, j)
            qh = q[:, at]
            total = attn[:, at] + dot(jnp.concatenate([qh, qh], axis=1), halves(state(0, mine, j), 0), NN)
            attn[:, at] = total
            squares = squares + total * total
            products = products + total * g[:, at]

    ones = jnp.ones((8, 3 * DK), BF16)

    def row_sums(array):
        high = array.astype(BF16)
        rest = array - high.astype(F32)
        middle = rest.astype(BF16)
        low = (rest - middle.astype(F32)).astype(BF16)
        return dot(ones, jnp.concatenate([high, middle, low], axis=1), NT)

    for i, array in enumerate((squares, products)):
        sums = row_sums(array)
        for j in range(4):
            zsend[pl.ds(4 * i + j, 1), :] = sums[0:1, j * DK : (j + 1) * DK]
    hear(2)
    for step in (8, 7, 9, 6, 10, 5, 11, 4, 12, 3, 13, 2, 14, 1, 15):
        zmessage(step).start()

    totals = zsend[...]
    for step in (1, 15, 2, 14, 3, 13, 4, 12, 5, 11, 6, 10, 7, 9, 8):
        zmessage(step).wait_recv()
        totals = totals + zrecv[step - 1]
    means = totals / FEATURES
    rms = jnp.sqrt(means[0:4] + 1e-05)
    inverse = 1.0 / rms
    weight = means[4:8] * inverse * inverse
    columns = jnp.concatenate([inverse, weight], axis=0).T
    for j in range(4):
        at = pl.ds(j * DK, DK)
        delta = (g[at, :] - attn[at, :] * columns[:, 4 + j : 5 + j]) * columns[:, j : j + 1]
        e[at, :] = delta.astype(BF16)

    for mine in (False, True):
        for j in range(2):
            at = half_head(c if mine else 1 - c, j)
            own[1, at] = dot(qt[at, :], e[:, at], NN)
            if not mine:
                sib_message(1, j).start()
    sib_message(1, 2).start()
    start_first(1)
    for j in range(4):
        at = pl.ds(j * DK, DK)
        normed[at, :] = (attn[at, :] * columns[:, j : j + 1] * gains).astype(BF16)

    def outer(h, carry):
        at = pl.ds(pl.multiple_of(h * DK, DK), DK)
        for r in range(4):
            low, rest = pl.ds(r * DK, DK), ROWS - r * DK
            strip = causal(dot(v[low, at], e[pl.ds(r * DK, rest), at], NT), False)
            dk_part[low, at] = dot(strip, q[pl.ds(r * DK, rest), at], NN)
            dv_part[low, at] = dot(scores_t[h, low, pl.ds(r * DK, rest)], e[pl.ds(r * DK, rest), at], NN)
        return carry

    lax.fori_loop(0, HEADS_HERE, outer, 0)
    start_second(1)

    for mine in (True, False):
        for j in range(2):
            at = half_head(c if mine else 1 - c, j)
            back = halves(state(0, mine, j), 1)
            for r in range(4):
                low = pl.ds(r * DK, DK)
                eh = e[low, at]
                strip = causal(dot(eh, v[pl.ds(0, (r + 1) * DK), at], NT), True)
                total = dot(strip, k[pl.ds(0, (r + 1) * DK), at], NN)
                dq[low, at] = (total + dot(jnp.concatenate([eh, eh], axis=1), back, NT)).astype(BF16)
    start_third(1)
    sib_message(1, 2).wait_recv()
    for mine in (True, False):
        for j in range(2):
            if not mine:
                pref_message(1, j).wait_recv()
            later[half_head(c if mine else 1 - c, j)] = state(1, mine, j)

    for way in range(2):
        for j in range(3):
            sib_message(way, j).wait_send()
        for j in range(2):
            pref_message(way, j).wait_send()
            for phase in range(2):
                for a in range(2):
                    for step in range(1, SIDE):
                        plane_message(way, phase, j, a, step).wait_send()
    for step in range(1, DEPTH):
        zmessage(step).wait_send()


def finish(
    normed, dq, dk_part, dv_part, later, k, v,
    normed_hbm, dq_hbm, dk_hbm, dv_hbm,
    dk, dv, store_sem,
):
    stores = [
        pltpu.make_async_copy(normed, normed_hbm, store_sem.at[0]),
        pltpu.make_async_copy(dq, dq_hbm, store_sem.at[1]),
    ]
    for store in stores:
        store.start()
    for h in range(HEADS_HERE):
        at = head(h)
        back = later[at]
        vh, kh = v[:, at], k[:, at]
        total = dk_part[:, at] + dot(jnp.concatenate([vh, vh], axis=1), halves(back, 1), NT)
        dk[:, at] = total.astype(BF16)
        total = dv_part[:, at] + dot(jnp.concatenate([kh, kh], axis=1), halves(back, 0), NN)
        dv[:, at] = total.astype(BF16)
        for i, (src, dst) in enumerate(((dk, dk_hbm), (dv, dv_hbm))):
            store = pltpu.make_async_copy(src.at[:, at], dst.at[:, at], store_sem.at[2 + 2 * h + i])
            store.start()
            stores.append(store)
    for store in stores:
        store.wait()


def shards(queries, keys, values, gain, d_out):
    width = HEADS_HERE * DK
    block = pltpu.VMEM((ROWS, width), BF16)
    wide = pltpu.VMEM((ROWS, width), F32)
    states = pltpu.VMEM((width, DK), F32)
    in_hbm = pl.BlockSpec(memory_space=pltpu.HBM)
    in_vmem = pl.BlockSpec(memory_space=pltpu.VMEM)
    arguments = (queries, keys, values, gain.reshape(1, width), d_out)
    partial = pl.pallas_call(
        body,
        out_shape=[block, block, wide, wide, states, block, block],
        in_specs=[in_hbm] * 5,
        out_specs=[in_vmem] * 7,
        scratch_shapes=[
            block, block, pltpu.VMEM((1, width), BF16),
            pltpu.VMEM((width, ROWS), BF16),
            pltpu.VMEM((HEADS_HERE, ROWS, ROWS), BF16),
            wide, wide, block,
            pltpu.VMEM((2, width, DK), F32),
            pltpu.VMEM((2, 2, 256, DK), F32),
            pltpu.VMEM((2, 2, 2, 64, DK), F32),
            pltpu.VMEM((2, 2, 2, 3, 64, DK), F32),
            pltpu.VMEM((2, 2, 64, DK), F32),
            pltpu.VMEM((2, 2, 2, 64, DK), F32),
            pltpu.VMEM((2, 2, 2, 3, 64, DK), F32),
            pltpu.VMEM((2, width, DK), F32),
            pltpu.VMEM((8, DK), F32),
            pltpu.VMEM((DEPTH - 1, 8, DK), F32),
            pltpu.SemaphoreType.DMA((5,)),
            pltpu.SemaphoreType.DMA((2, 29)),
            pltpu.SemaphoreType.DMA((2, 29)),
            pltpu.SemaphoreType.DMA((DEPTH - 1,)),
            pltpu.SemaphoreType.DMA((DEPTH - 1,)),
            pltpu.SemaphoreType.REGULAR((3,)),
        ],
        compiler_params=pltpu.CompilerParams(
            collective_id=0, has_side_effects=True, vmem_limit_bytes=32 * 1024 * 1024
        ),
        name="attention",
    )(*[pltpu.with_memory_space_constraint(array, pltpu.HBM) for array in arguments])
    return pl.pallas_call(
        finish,
        out_shape=[jax.ShapeDtypeStruct((ROWS, width), BF16)] * 4,
        in_specs=[in_vmem] * 7,
        out_specs=[in_hbm] * 4,
        scratch_shapes=[block, block, pltpu.SemaphoreType.DMA((10,))],
        compiler_params=pltpu.CompilerParams(vmem_limit_bytes=16 * 1024 * 1024),
        name="finish",
    )(*[pltpu.with_memory_space_constraint(array, pltpu.VMEM) for array in partial])


def solution(mesh):
    in_specs = (P("seq", "head"), P("seq", "head"), P("seq", "head"), P("head"), P("seq", "head"))
    out_specs = (P("seq", "head"), P("seq", "head"), P("seq", "head"), P("seq", "head"))
    return jax.shard_map(shards, mesh=mesh, in_specs=in_specs, out_specs=out_specs, check_vma=False)
```

time: 61.8 us -> 51.5 us (0.83)
  local copies, waits for them, and re-layouts: 7.34 us -> 1.26 us
  Pallas kernels: 52.9 us -> 49.4 us
  other arithmetic: 0.68 us -> 0 us
    unnamed x12 -> x0, local copies, waits for them, and re-layouts: 7.34 us -> none
    pallas_call x1 -> x2, Pallas kernels: 52.9 us -> 49.4 us  [the longest x1 47.9 us: shards(): pl.pallas_call(body, out_shape=[block, block, wide, wide, states, block,...]
    reshape x0 -> x1, local copies, waits for them, and re-layouts: none -> 1.26 us  [shards(): arguments = (queries, keys, values, gain.reshape(1, width), d_out)]
    reshape x1 -> x0, other arithmetic: 0.68 us -> none  [shards(): gain.astype(F32).reshape(1, HEADS_HERE * DK)]
where the time goes in v2:
time: 51.5 us; the launch traced here: 51.3 us
  Pallas kernels  49.4 us (96%)
  local copies, waits for them, and re-layouts  1.26 us (2%)
  between operations  0.64 us (1%)
    pallas_call x1, Pallas kernels, shards(): pl.pallas_call(body, out_shape=[block, block, wide, wide, states, block,...  47.9 us
    pallas_call x1, Pallas kernels, shards(): pl.pallas_call(finish, out_shape=[jax.ShapeDtypeStruct((ROWS, width), BF1...  1.51 us
    reshape x1, local copies, waits for them, and re-layouts, shards(): arguments = (queries, keys, values, gain.reshape(1, width), d_out)  1.26 us

profile of v2, /device:TPU:1, one launch (start us, length us, event | category | flops | bytes accessed | tf_op | source)
XLA Modules:
  0.0 51.3 jit_solution(11681728365235321662)
XLA Ops:
  0.6 1.3 %reshape.11.gain_hbm = bf16[1,512]{1,0:T(2,128)(2,1)} reshape(bf16[512]{0:T(512)(128)(2,1)} %param.8) | data formatting | bytes 2048 | tf_op jit(solution)/shard_map/reshape | solution.py:373
  1.9 47.9 %attention.1 = (bf16[512,512]{1,0:T(8,128)(2,1)S(1)}, bf16[512,512]{1,0:T(8,128)(2,1)S(1)}, f32[512,512]{1,0:T(8,128)S(1)}, f32[512,512]{1,0:T(8,128)S(1)}, f32[...) custom-call(bf16[512,512]{1,0:T(8,128)(2,1)} %q_hbm.1, bf16[512,512]{1,0:T(8,128)(2,1)} %k_hbm.1, ...), custom_call_target="tpu_custom_call" | custom-call | tf_op jit(solution)/shard_map/attention/pallas_call | solution.py:374
  49.8 1.5 %finish.1 = (bf16[512,512]{1,0:T(8,128)(2,1)}, bf16[512,512]{1,0:T(8,128)(2,1)}, bf16[512,512]{1,0:T(8,128)(2,1)}, bf16[512,512]{1,0:T(8,128)(2,1)}) custom-call(bf16[512,512]{1,0:T(8,128)(2,1)S(1)} %get-tuple-element.11.normed, bf16[512,512]{1,0:T(8,128)(2,1)S(1)} %get-tuple-element.12.dq, f32[512,512]{1,0:T(8,128)S(1)} %get-tuple-element.13.dk_part, ...), custom_call_target="tpu_custom_call" | custom-call | tf_op jit(solution)/shard_map/finish/pallas_call | solution.py:406

commit v3 on v2

--- a/solution.py
+++ b/solution.py
@@ -38,10 +38,10 @@
 
 def body(
     q_hbm, k_hbm, v_hbm, gain_hbm, d_hbm,
-    normed, dq, dk_part, dv_part, later, k, v,
+    normed, dq, dk, dv, dk_part, dv_part, later, k, v,
     q, d, gain,
-    qt, scores_t, attn, g, e,
-    own, sib, chip, recv1, row, cols, recv2, pref,
+    qt, scores_t, attn, g, e, inverses, weights,
+    own, sib, chip, recv1, row, cols, local, base, recv2, pref,
     zsend, zrecv,
     load_sem, send_sem, recv_sem, zsend_sem, zrecv_sem, near_sem,
 ):
@@ -51,10 +51,10 @@
     sibling = (s + 1 - 2 * c, z)
 
     def along_y(step):
-        return (x * 8 + ((y + step) % SIDE) * 2 + c, z)
+        return (x * 8 + ((y + step) % SIDE) * 2 + 1 - c, z)
 
     def along_x(step):
-        return (((x + step) % SIDE) * 8 + y * 2 + c, z)
+        return (((x + step) % SIDE) * 8 + y * 2 + 1 - c, z)
 
     def along_z(step):
         return (s, (z + step) % DEPTH)
@@ -63,7 +63,7 @@
         pltpu.make_async_copy(src, dst, load_sem.at[i])
         for i, (src, dst) in enumerate(((k_hbm, k), (v_hbm, v), (q_hbm, q), (d_hbm, d), (gain_hbm, gain)))
     ]
-    for load in loads:
+    for load in loads[:2]:
         load.start()
 
     barrier = pltpu.get_barrier_semaphore()
@@ -96,8 +96,11 @@
     def pref_message(way, j):
         return message(way, 3 + j, pref.at[way, half_head(c, j)], pref.at[way, half_head(c, j)], sibling)
 
+    def base_message(way, j):
+        return message(way, 5 + j, local.at[way, j], base.at[way, j], sibling)
+
     def plane_message(way, phase, j, a, step):
-        number = 5 + ((phase * 2 + j) * 2 + a) * 3 + step - 1
+        number = 7 + ((phase * 2 + j) * 2 + a) * 3 + step - 1
         device = along_y(step) if phase == a else along_x(step)
         if phase == 0:
             src, dst = chip.at[way, j, a], recv1.at[way, j, a, step - 1]
@@ -133,7 +136,9 @@
             for a in range(2):
                 for step in range(1, SIDE):
                     plane_message(way, 0, j, a, step).wait_recv()
-                mine = chip[way, j, a]
+                if j + a == 0:
+                    sib_message(way, 2).wait_recv()
+                mine = own[way, pl.ds(256 * (1 - c) + j * DK + 64 * a, 64)] + sib[way, 1, pl.ds(j * DK + 64 * a, 64)]
                 if a == 0:
                     total, before = mine, jnp.zeros_like(mine)
                     for step in range(1, SIDE):
@@ -141,31 +146,29 @@
                         total = total + block
                         before = before + jnp.where(counts(way, step, y), block, 0.0)
                     row[way, j] = total
-                    pref[way, pl.ds(256 * c + j * DK, 64)] = before
+                    local[way, j, pl.ds(0, 64)] = before
                 else:
                     column = jnp.zeros_like(mine)
                     for step in range(1, SIDE):
                         column = column + jnp.where(counts(way, step, x), recv1[way, j, a, step - 1], 0.0)
                     cols[way, j, 0] = column
+                    local[way, j, pl.ds(64, 64)] = column
                     cols[way, j, 1] = column + mine
                 for step in (2, 1, 3):
                     plane_message(way, 1, j, a, step).start()
+            base_message(way, j).start()
 
     def start_third(way):
         for j in range(2):
+            base_message(way, j).wait_recv()
             for a in range(2):
                 for step in range(1, SIDE):
                     plane_message(way, 1, j, a, step).wait_recv()
-                at = pl.ds(256 * c + j * DK + 64 * a, 64)
-                if a == 0:
-                    total = pref[way, at]
-                    for step in range(1, SIDE):
-                        total = total + jnp.where(counts(way, step, x), recv2[way, j, a, step - 1], 0.0)
-                else:
-                    total = cols[way, j, 0]
-                    for step in range(1, SIDE):
-                        total = total + recv2[way, j, a, step - 1]
-                pref[way, at] = total
+                total = base[way, j, pl.ds(64 * a, 64)]
+                for step in range(1, SIDE):
+                    block = recv2[way, j, a, step - 1]
+                    total = total + (jnp.where(counts(way, step, x), block, 0.0) if a == 0 else block)
+                pref[way, pl.ds(256 * c + j * DK + 64 * a, 64)] = total
             pref_message(way, j).start()
 
     def state(way, mine, j):
@@ -191,6 +194,8 @@
 
     loads[0].wait()
     loads[1].wait()
+    for load in loads[2:]:
+        load.start()
     for j in range(2):
         at = half_head(1 - c, j)
         own[0, at] = dot(k[:, at], v[:, at], TN)
@@ -219,8 +224,6 @@
     tell(1)
     start_second(0)
 
-    gains = gain[...].astype(F32)
-
     def prepare(h, carry):
         at = pl.ds(pl.multiple_of(h * DK, DK), DK)
         qt[at, :] = q[:, at].astype(F32).T.astype(BF16)
@@ -231,11 +234,11 @@
         return carry
 
     lax.fori_loop(0, HEADS_HERE, prepare, 0)
-    g[...] = d[...].astype(F32) * gains
+    for h in range(HEADS_HERE):
+        g[:, head(h)] = d[:, head(h)].astype(F32) * gain[h : h + 1, :].astype(F32)
     hear(1)
     tell(2)
     start_third(0)
-    sib_message(0, 2).wait_recv()
 
     squares = jnp.zeros((ROWS, DK), F32)
     products = jnp.zeros((ROWS, DK), F32)
@@ -277,21 +280,20 @@
     weight = means[4:8] * inverse * inverse
     columns = jnp.concatenate([inverse, weight], axis=0).T
     for j in range(4):
-        at = pl.ds(j * DK, DK)
-        delta = (g[at, :] - attn[at, :] * columns[:, 4 + j : 5 + j]) * columns[:, j : j + 1]
-        e[at, :] = delta.astype(BF16)
-
+        inverses[pl.ds(j * DK, DK), :] = jnp.broadcast_to(columns[:, j : j + 1], (DK, DK))
+        weights[pl.ds(j * DK, DK), :] = jnp.broadcast_to(columns[:, 4 + j : 5 + j], (DK, DK))
     for mine in (False, True):
         for j in range(2):
             at = half_head(c if mine else 1 - c, j)
-            own[1, at] = dot(qt[at, :], e[:, at], NN)
+            delta = ((g[:, at] - attn[:, at] * weights[...]) * inverses[...]).astype(BF16)
+            e[:, at] = delta
+            own[1, at] = dot(qt[at, :], delta, NN)
             if not mine:
                 sib_message(1, j).start()
     sib_message(1, 2).start()
     start_first(1)
-    for j in range(4):
-        at = pl.ds(j * DK, DK)
-        normed[at, :] = (attn[at, :] * columns[:, j : j + 1] * gains).astype(BF16)
+    for h in range(HEADS_HERE):
+        normed[:, head(h)] = (attn[:, head(h)] * inverses[...] * gain[h : h + 1, :].astype(F32)).astype(BF16)
 
     def outer(h, carry):
         at = pl.ds(pl.multiple_of(h * DK, DK), DK)
@@ -316,18 +318,21 @@
                 total = dot(strip, k[pl.ds(0, (r + 1) * DK), at], NN)
                 dq[low, at] = (total + dot(jnp.concatenate([eh, eh], axis=1), back, NT)).astype(BF16)
     start_third(1)
-    sib_message(1, 2).wait_recv()
     for mine in (True, False):
         for j in range(2):
-            if not mine:
+            at = half_head(c if mine else 1 - c, j)
+            if mine:
+                last_products(at, state(1, mine, j), k, v, dk_part, dv_part, dk, dv)
+            else:
                 pref_message(1, j).wait_recv()
-            later[half_head(c if mine else 1 - c, j)] = state(1, mine, j)
+                later[pl.ds(j * DK, DK)] = state(1, mine, j)
 
     for way in range(2):
         for j in range(3):
             sib_message(way, j).wait_send()
         for j in range(2):
             pref_message(way, j).wait_send()
+            base_message(way, j).wait_send()
             for phase in range(2):
                 for a in range(2):
                     for step in range(1, SIDE):
@@ -336,64 +341,76 @@
         zmessage(step).wait_send()
 
 
+def last_products(at, back, k, v, dk_part, dv_part, dk, dv):
+    vh, kh = v[:, at], k[:, at]
+    total = dk_part[:, at] + dot(jnp.concatenate([vh, vh], axis=1), halves(back, 1), NT)
+    dk[:, at] = total.astype(BF16)
+    total = dv_part[:, at] + dot(jnp.concatenate([kh, kh], axis=1), halves(back, 0), NN)
+    dv[:, at] = total.astype(BF16)
+
+
 def finish(
-    normed, dq, dk_part, dv_part, later, k, v,
+    normed, dq, dk_mine, dv_mine, dk_part, dv_part, later, k, v,
     normed_hbm, dq_hbm, dk_hbm, dv_hbm,
     dk, dv, store_sem,
 ):
-    stores = [
-        pltpu.make_async_copy(normed, normed_hbm, store_sem.at[0]),
-        pltpu.make_async_copy(dq, dq_hbm, store_sem.at[1]),
-    ]
-    for store in stores:
-        store.start()
-    for h in range(HEADS_HERE):
-        at = head(h)
-        back = later[at]
-        vh, kh = v[:, at], k[:, at]
-        total = dk_part[:, at] + dot(jnp.concatenate([vh, vh], axis=1), halves(back, 1), NT)
-        dk[:, at] = total.astype(BF16)
-        total = dv_part[:, at] + dot(jnp.concatenate([kh, kh], axis=1), halves(back, 0), NN)
-        dv[:, at] = total.astype(BF16)
-        for i, (src, dst) in enumerate(((dk, dk_hbm), (dv, dv_hbm))):
-            store = pltpu.make_async_copy(src.at[:, at], dst.at[:, at], store_sem.at[2 + 2 * h + i])
-            store.start()
-            stores.append(store)
-    for store in stores:
-        store.wait()
+    c = lax.axis_index("seq") % 2
+    stores = []
+
+    def store(src, dst):
+        copy = pltpu.make_async_copy(src, dst, store_sem.at[len(stores)])
+        copy.start()
+        stores.append(copy)
+
+    here = pl.ds(pl.multiple_of(256 * c, 256), 256)
+    store(dk_mine.at[:, here], dk_hbm.at[:, here])
+    store(dv_mine.at[:, here], dv_hbm.at[:, here])
+    for part in range(2):
+        rows = pl.ds(256 * part, 256)
+        store(normed.at[rows], normed_hbm.at[rows])
+        store(dq.at[rows], dq_hbm.at[rows])
+    for j in range(2):
+        at = pl.ds(pl.multiple_of((2 * (1 - c) + j) * DK, DK), DK)
+        last_products(at, later[pl.ds(j * DK, DK)], k, v, dk_part, dv_part, dk, dv)
+        store(dk.at[:, at], dk_hbm.at[:, at])
+        store(dv.at[:, at], dv_hbm.at[:, at])
+    for copy in stores:
+        copy.wait()
 
 
 def shards(queries, keys, values, gain, d_out):
     width = HEADS_HERE * DK
     block = pltpu.VMEM((ROWS, width), BF16)
     wide = pltpu.VMEM((ROWS, width), F32)
-    states = pltpu.VMEM((width, DK), F32)
+    states = pltpu.VMEM((256, DK), F32)
     in_hbm = pl.BlockSpec(memory_space=pltpu.HBM)
     in_vmem = pl.BlockSpec(memory_space=pltpu.VMEM)
-    arguments = (queries, keys, values, gain.reshape(1, width), d_out)
+    arguments = (queries, keys, values, gain.reshape(HEADS_HERE, DK), d_out)
     partial = pl.pallas_call(
         body,
-        out_shape=[block, block, wide, wide, states, block, block],
+        out_shape=[block, block, block, block, wide, wide, states, block, block],
         in_specs=[in_hbm] * 5,
-        out_specs=[in_vmem] * 7,
+        out_specs=[in_vmem] * 9,
         scratch_shapes=[
-            block, block, pltpu.VMEM((1, width), BF16),
+            block, block, pltpu.VMEM((HEADS_HERE, DK), BF16),
             pltpu.VMEM((width, ROWS), BF16),
             pltpu.VMEM((HEADS_HERE, ROWS, ROWS), BF16),
-            wide, wide, block,
+            wide, wide, block, pltpu.VMEM((ROWS, DK), F32), pltpu.VMEM((ROWS, DK), F32),
             pltpu.VMEM((2, width, DK), F32),
             pltpu.VMEM((2, 2, 256, DK), F32),
             pltpu.VMEM((2, 2, 2, 64, DK), F32),
             pltpu.VMEM((2, 2, 2, 3, 64, DK), F32),
             pltpu.VMEM((2, 2, 64, DK), F32),
             pltpu.VMEM((2, 2, 2, 64, DK), F32),
+            pltpu.VMEM((2, 2, DK, DK), F32),
+            pltpu.VMEM((2, 2, DK, DK), F32),
             pltpu.VMEM((2, 2, 2, 3, 64, DK), F32),
             pltpu.VMEM((2, width, DK), F32),
             pltpu.VMEM((8, DK), F32),
             pltpu.VMEM((DEPTH - 1, 8, DK), F32),
             pltpu.SemaphoreType.DMA((5,)),
-            pltpu.SemaphoreType.DMA((2, 29)),
-            pltpu.SemaphoreType.DMA((2, 29)),
+            pltpu.SemaphoreType.DMA((2, 31)),
+            pltpu.SemaphoreType.DMA((2, 31)),
             pltpu.SemaphoreType.DMA((DEPTH - 1,)),
             pltpu.SemaphoreType.DMA((DEPTH - 1,)),
             pltpu.SemaphoreType.REGULAR((3,)),
@@ -406,7 +423,7 @@
     return pl.pallas_call(
         finish,
         out_shape=[jax.ShapeDtypeStruct((ROWS, width), BF16)] * 4,
-        in_specs=[in_vmem] * 7,
+        in_specs=[in_vmem] * 9,
         out_specs=[in_hbm] * 4,
         scratch_shapes=[block, block, pltpu.SemaphoreType.DMA((10,))],
         compiler_params=pltpu.CompilerParams(vmem_limit_bytes=16 * 1024 * 1024),

time: 51.5 us -> 50 us (0.971)
  local copies, waits for them, and re-layouts: 1.26 us -> 0 us
    reshape x1 -> x0, local copies, waits for them, and re-layouts: 1.26 us -> none  [shards(): arguments = (queries, keys, values, gain.reshape(1, width), d_out)]
where the time goes in v3:
time: 50 us; the launch traced here: 49.9 us
  Pallas kernels  49.2 us (98%)
  between operations  0.64 us (1%)
    pallas_call x1, Pallas kernels, shards(): pl.pallas_call(body, out_shape=[block, block, block, block, wide, wide, s...  47.7 us
    pallas_call x1, Pallas kernels, shards(): pl.pallas_call(finish, out_shape=[jax.ShapeDtypeStruct((ROWS, width), BF1...  1.57 us

profile of v3, /device:TPU:1, one launch (start us, length us, event | category | flops | bytes accessed | tf_op | source)
XLA Modules:
  0.0 49.9 jit_solution(15045222212899313606)
XLA Ops:
  0.6 47.7 %attention.1 = (bf16[512,512]{1,0:T(8,128)(2,1)S(1)}, bf16[512,512]{1,0:T(8,128)(2,1)S(1)}, bf16[512,512]{1,0:T(8,128)(2,1)S(1)}, bf16[512,512]{1,0:T(8,128)(2,1...) custom-call(bf16[512,512]{1,0:T(8,128)(2,1)} %q_hbm.1, ...), custom_call_target="tpu_custom_call" | custom-call | tf_op jit(solution)/shard_map/attention/pallas_call | solution.py:389
  48.3 1.6 %finish.1 = (bf16[512,512]{1,0:T(8,128)(2,1)}, bf16[512,512]{1,0:T(8,128)(2,1)}, bf16[512,512]{1,0:T(8,128)(2,1)}, bf16[512,512]{1,0:T(8,128)(2,1)}) custom-call(bf16[512,512]{1,0:T(8,128)(2,1)S(1)} %get-tuple-element.13.normed, bf16[512,512]{1,0:T(8,128)(2,1)S(1)} %get-tuple-element.14.dq, bf16[512,512]{1,0:T(8,128)(2,1)S(1)} %get-tuple-element.15.dk_mine, ...), custom_call_target="tpu_custom_call" | custom-call | tf_op jit(solution)/shard_map/finish/pallas_call | solution.py:423

commit v4 on v3

--- a/solution.py
+++ b/solution.py
@@ -59,11 +59,22 @@
     def along_z(step):
         return (s, (z + step) % DEPTH)
 
+    here, there = pl.ds(pl.multiple_of(256 * c, 256), 256), pl.ds(pl.multiple_of(256 - 256 * c, 256), 256)
     loads = [
         pltpu.make_async_copy(src, dst, load_sem.at[i])
-        for i, (src, dst) in enumerate(((k_hbm, k), (v_hbm, v), (q_hbm, q), (d_hbm, d), (gain_hbm, gain)))
+        for i, (src, dst) in enumerate(
+            (
+                (k_hbm.at[:, there], k.at[:, there]),
+                (v_hbm.at[:, there], v.at[:, there]),
+                (k_hbm.at[:, here], k.at[:, here]),
+                (v_hbm.at[:, here], v.at[:, here]),
+                (q_hbm, q),
+                (d_hbm, d),
+                (gain_hbm, gain),
+            )
+        )
     ]
-    for load in loads[:2]:
+    for load in loads[:4]:
         load.start()
 
     barrier = pltpu.get_barrier_semaphore()
@@ -121,24 +132,46 @@
     def counts(way, step, place):
         return step <= place if way == 0 else step > place
 
+    def start_plane(way, phase, j, a):
+        for step in (2, 1, 3):
+            if phase == a:
+                plane_message(way, phase, j, a, step).start()
+            else:
+                pl.when(reaches(way, step))(plane_message(way, phase, j, a, step).start)
+
+    def wait_plane(way, phase, j, a):
+        for step in range(1, SIDE):
+            if phase == a:
+                plane_message(way, phase, j, a, step).wait_recv()
+            else:
+                pl.when(counts(way, step, x))(plane_message(way, phase, j, a, step).wait_recv)
+
+    def leave_plane(way, phase, j, a):
+        for step in range(1, SIDE):
+            if phase == a:
+                plane_message(way, phase, j, a, step).wait_send()
+            else:
+                pl.when(reaches(way, step))(plane_message(way, phase, j, a, step).wait_send)
+
+    def reaches(way, step):
+        return x + step < SIDE if way == 0 else x + step >= SIDE
+
     def start_first(way):
         for j in range(2):
             sib_message(way, j).wait_recv()
             total = own[way, half_head(c, j)] + sib[way, 0, pl.ds(j * DK, DK)]
             for a in range(2):
                 chip[way, j, a] = total[64 * a : 64 * a + 64]
-            for step in (2, 1, 3):
-                for a in range(2):
-                    plane_message(way, 0, j, a, step).start()
+            for a in range(2):
+                start_plane(way, 0, j, a)
 
     def start_second(way):
-        for j in range(2):
-            for a in range(2):
-                for step in range(1, SIDE):
-                    plane_message(way, 0, j, a, step).wait_recv()
-                if j + a == 0:
-                    sib_message(way, 2).wait_recv()
-                mine = own[way, pl.ds(256 * (1 - c) + j * DK + 64 * a, 64)] + sib[way, 1, pl.ds(j * DK + 64 * a, 64)]
+        sib_message(way, 2).wait_recv()
+        for a in (1, 0):
+            for j in range(2):
+                wait_plane(way, 0, j, a)
+                rows = pl.ds(j * DK + 64 * a, 64)
+                mine = own[way, pl.ds(256 * (1 - c) + j * DK + 64 * a, 64)] + sib[way, 1, rows]
                 if a == 0:
                     total, before = mine, jnp.zeros_like(mine)
                     for step in range(1, SIDE):
@@ -152,18 +185,17 @@
                     for step in range(1, SIDE):
                         column = column + jnp.where(counts(way, step, x), recv1[way, j, a, step - 1], 0.0)
                     cols[way, j, 0] = column
+                    cols[way, j, 1] = column + mine
                     local[way, j, pl.ds(64, 64)] = column
-                    cols[way, j, 1] = column + mine
-                for step in (2, 1, 3):
-                    plane_message(way, 1, j, a, step).start()
-            base_message(way, j).start()
+                start_plane(way, 1, j, a)
+                if a == 0:
+                    base_message(way, j).start()
 
     def start_third(way):
         for j in range(2):
             base_message(way, j).wait_recv()
             for a in range(2):
-                for step in range(1, SIDE):
-                    plane_message(way, 1, j, a, step).wait_recv()
+                wait_plane(way, 1, j, a)
                 total = base[way, j, pl.ds(64 * a, 64)]
                 for step in range(1, SIDE):
                     block = recv2[way, j, a, step - 1]
@@ -192,9 +224,9 @@
             [jnp.where(keep, block[:, :DK], 0.0).astype(BF16), block[:, DK:].astype(BF16)], axis=1
         )
 
-    loads[0].wait()
-    loads[1].wait()
-    for load in loads[2:]:
+    for load in loads[:2]:
+        load.wait()
+    for load in loads[4:]:
         load.start()
     for j in range(2):
         at = half_head(1 - c, j)
@@ -203,13 +235,14 @@
     tell(0)
     for j in range(2):
         sib_message(0, j).start()
+    for load in loads[2:4]:
+        load.wait()
     for j in range(2):
         at = half_head(c, j)
         own[0, at] = dot(k[:, at], v[:, at], TN)
     sib_message(0, 2).start()
-    loads[2].wait()
-    loads[3].wait()
-    loads[4].wait()
+    for load in loads[4:]:
+        load.wait()
     start_first(0)
 
     def inner(h, carry):
@@ -335,8 +368,7 @@
             base_message(way, j).wait_send()
             for phase in range(2):
                 for a in range(2):
-                    for step in range(1, SIDE):
-                        plane_message(way, phase, j, a, step).wait_send()
+                    leave_plane(way, phase, j, a)
     for step in range(1, DEPTH):
         zmessage(step).wait_send()
 
@@ -408,7 +440,7 @@
             pltpu.VMEM((2, width, DK), F32),
             pltpu.VMEM((8, DK), F32),
             pltpu.VMEM((DEPTH - 1, 8, DK), F32),
-            pltpu.SemaphoreType.DMA((5,)),
+            pltpu.SemaphoreType.DMA((7,)),
             pltpu.SemaphoreType.DMA((2, 31)),
             pltpu.SemaphoreType.DMA((2, 31)),
             pltpu.SemaphoreType.DMA((DEPTH - 1,)),

time: 50 us -> 50.7 us (1.014)
  Pallas kernels: 49.2 us -> 50 us
    pallas_call x1, Pallas kernels: 47.7 us -> 48.4 us  [shards(): pl.pallas_call(body, out_shape=[block, block, block, block, wide, wide, s...]
where the time goes in v4:
time: 50.7 us; the launch traced here: 50.6 us
  Pallas kernels  50 us (99%)
  between operations  0.64 us (1%)
    pallas_call x1, Pallas kernels, shards(): pl.pallas_call(body, out_shape=[block, block, block, block, wide, wide, s...  48.4 us
    pallas_call x1, Pallas kernels, shards(): pl.pallas_call(finish, out_shape=[jax.ShapeDtypeStruct((ROWS, width), BF1...  1.56 us

profile of v4, /device:TPU:1, one launch (start us, length us, event | category | flops | bytes accessed | tf_op | source)
XLA Modules:
  0.0 50.6 jit_solution(10020220373507569779)
XLA Ops:
  0.6 48.4 %attention.1 = (bf16[512,512]{1,0:T(8,128)(2,1)S(1)}, bf16[512,512]{1,0:T(8,128)(2,1)S(1)}, bf16[512,512]{1,0:T(8,128)(2,1)S(1)}, bf16[512,512]{1,0:T(8,128)(2,1...) custom-call(bf16[512,512]{1,0:T(8,128)(2,1)} %q_hbm.1, ...), custom_call_target="tpu_custom_call" | custom-call | tf_op jit(solution)/shard_map/attention/pallas_call | solution.py:421
  49.0 1.6 %finish.1 = (bf16[512,512]{1,0:T(8,128)(2,1)}, bf16[512,512]{1,0:T(8,128)(2,1)}, bf16[512,512]{1,0:T(8,128)(2,1)}, bf16[512,512]{1,0:T(8,128)(2,1)}) custom-call(bf16[512,512]{1,0:T(8,128)(2,1)S(1)} %get-tuple-element.13.normed, bf16[512,512]{1,0:T(8,128)(2,1)S(1)} %get-tuple-element.14.dq, bf16[512,512]{1,0:T(8,128)(2,1)S(1)} %get-tuple-element.15.dk_mine, ...), custom_call_target="tpu_custom_call" | custom-call | tf_op jit(solution)/shard_map/finish/pallas_call | solution.py:455

commit v5 on v4

--- a/solution.py
+++ b/solution.py
@@ -10,6 +10,9 @@
 DK = 128
 ROWS = 512
 HEADS_HERE = 4
+PIECES = 4
+PIECE = 256 // PIECES
+PART = PIECE // 2
 FEATURES = 8192
 SIDE = 4
 DEPTH = 16
@@ -43,7 +46,7 @@
     qt, scores_t, attn, g, e, inverses, weights,
     own, sib, chip, recv1, row, cols, local, base, recv2, pref,
     zsend, zrecv,
-    load_sem, send_sem, recv_sem, zsend_sem, zrecv_sem, near_sem,
+    load_sem, send_sem, sib_sem, pref_sem, base_sem, plane_sem, zsend_sem, zrecv_sem, near_sem,
 ):
     s = lax.axis_index("seq")
     z = lax.axis_index("head")
@@ -93,115 +96,103 @@
     def half_head(half, j):
         return pl.ds(pl.multiple_of((2 * half + j) * DK, DK), DK)
 
-    def message(way, number, src, dst, device):
+    def message(send, recv, src, dst, device):
         return pltpu.make_async_remote_copy(
-            src_ref=src, dst_ref=dst, send_sem=send_sem.at[way, number], recv_sem=recv_sem.at[way, number],
-            device_id=device, device_id_type=MESH,
+            src_ref=src, dst_ref=dst, send_sem=send, recv_sem=recv, device_id=device, device_id_type=MESH
         )
 
+    def wait_bytes(ref, sem):
+        pltpu.make_async_copy(ref, ref, sem).wait()
+
     def sib_message(way, j):
+        send, recv = send_sem.at[way, 0], sib_sem.at[way, j]
         if j == 2:
-            return message(way, 2, own.at[way, pl.ds(256 * c, 256)], sib.at[way, 1], sibling)
-        return message(way, j, own.at[way, half_head(1 - c, j)], sib.at[way, 0, pl.ds(j * DK, DK)], sibling)
-
-    def pref_message(way, j):
-        return message(way, 3 + j, pref.at[way, half_head(c, j)], pref.at[way, half_head(c, j)], sibling)
-
-    def base_message(way, j):
-        return message(way, 5 + j, local.at[way, j], base.at[way, j], sibling)
-
-    def plane_message(way, phase, j, a, step):
-        number = 7 + ((phase * 2 + j) * 2 + a) * 3 + step - 1
+            return message(send, recv, own.at[way, pl.ds(256 * c, 256)], sib.at[way, 1], sibling)
+        return message(send, recv, own.at[way, half_head(1 - c, j)], sib.at[way, 0, pl.ds(j * DK, DK)], sibling)
+
+    def piece(half, i):
+        return pl.ds(pl.multiple_of(256 * half + PIECE * i, PIECE), PIECE)
+
+    def pref_message(way, i):
+        send, recv = send_sem.at[way, 1], pref_sem.at[way, i // (PIECES // 2)]
+        return message(send, recv, pref.at[way, piece(c, i)], pref.at[way, piece(c, i)], sibling)
+
+    def base_message(way, i):
+        return message(send_sem.at[way, 2], base_sem.at[way], local.at[way, i], base.at[way, i], sibling)
+
+    def plane_message(way, phase, i, a, step):
         device = along_y(step) if phase == a else along_x(step)
         if phase == 0:
-            src, dst = chip.at[way, j, a], recv1.at[way, j, a, step - 1]
+            src, dst = chip.at[way, i, a], recv1.at[way, i, a, step - 1]
         elif a == 0:
-            src, dst = row.at[way, j], recv2.at[way, j, a, step - 1]
+            src, dst = row.at[way, i], recv2.at[way, i, a, step - 1]
         else:
             wrapped = (y + step) // SIDE
             pick = 1 - wrapped if way == 0 else wrapped
-            src, dst = cols.at[way, j, pick], recv2.at[way, j, a, step - 1]
-        return message(way, number, src, dst, device)
+            src, dst = cols.at[way, i, pick], recv2.at[way, i, a, step - 1]
+        return message(send_sem.at[way, 3 + phase], plane_sem.at[way, phase, i], src, dst, device)
 
     def zmessage(step):
-        return pltpu.make_async_remote_copy(
-            src_ref=zsend, dst_ref=zrecv.at[step - 1], send_sem=zsend_sem.at[step - 1],
-            recv_sem=zrecv_sem.at[step - 1], device_id=along_z(step), device_id_type=MESH,
-        )
+        return message(zsend_sem, zrecv_sem, zsend, zrecv.at[step - 1], along_z(step))
 
     def counts(way, step, place):
         return step <= place if way == 0 else step > place
 
-    def start_plane(way, phase, j, a):
+    def start_plane(way, phase, i):
         for step in (2, 1, 3):
-            if phase == a:
-                plane_message(way, phase, j, a, step).start()
-            else:
-                pl.when(reaches(way, step))(plane_message(way, phase, j, a, step).start)
-
-    def wait_plane(way, phase, j, a):
-        for step in range(1, SIDE):
-            if phase == a:
-                plane_message(way, phase, j, a, step).wait_recv()
-            else:
-                pl.when(counts(way, step, x))(plane_message(way, phase, j, a, step).wait_recv)
-
-    def leave_plane(way, phase, j, a):
-        for step in range(1, SIDE):
-            if phase == a:
-                plane_message(way, phase, j, a, step).wait_send()
-            else:
-                pl.when(reaches(way, step))(plane_message(way, phase, j, a, step).wait_send)
-
-    def reaches(way, step):
-        return x + step < SIDE if way == 0 else x + step >= SIDE
+            for a in range(2):
+                plane_message(way, phase, i, a, step).start()
 
     def start_first(way):
-        for j in range(2):
-            sib_message(way, j).wait_recv()
-            total = own[way, half_head(c, j)] + sib[way, 0, pl.ds(j * DK, DK)]
+        for i in range(PIECES):
+            if i % (PIECES // 2) == 0:
+                sib_message(way, i // (PIECES // 2)).wait_recv()
+            total = own[way, piece(c, i)] + sib[way, 0, pl.ds(PIECE * i, PIECE)]
             for a in range(2):
-                chip[way, j, a] = total[64 * a : 64 * a + 64]
-            for a in range(2):
-                start_plane(way, 0, j, a)
+                chip[way, i, a] = total[PART * a : PART * a + PART]
+            start_plane(way, 0, i)
 
     def start_second(way):
         sib_message(way, 2).wait_recv()
-        for a in (1, 0):
-            for j in range(2):
-                wait_plane(way, 0, j, a)
-                rows = pl.ds(j * DK + 64 * a, 64)
-                mine = own[way, pl.ds(256 * (1 - c) + j * DK + 64 * a, 64)] + sib[way, 1, rows]
-                if a == 0:
-                    total, before = mine, jnp.zeros_like(mine)
-                    for step in range(1, SIDE):
-                        block = recv1[way, j, a, step - 1]
-                        total = total + block
-                        before = before + jnp.where(counts(way, step, y), block, 0.0)
-                    row[way, j] = total
-                    local[way, j, pl.ds(0, 64)] = before
-                else:
-                    column = jnp.zeros_like(mine)
-                    for step in range(1, SIDE):
-                        column = column + jnp.where(counts(way, step, x), recv1[way, j, a, step - 1], 0.0)
-                    cols[way, j, 0] = column
-                    cols[way, j, 1] = column + mine
-                    local[way, j, pl.ds(64, 64)] = column
-                start_plane(way, 1, j, a)
-                if a == 0:
-                    base_message(way, j).start()
+        for i in range(PIECES):
+            wait_bytes(recv1.at[way, i], plane_sem.at[way, 0, i])
+            mine = own[way, piece(1 - c, i)] + sib[way, 1, pl.ds(PIECE * i, PIECE)]
+            total, before = mine[:PART], jnp.zeros((PART, DK), F32)
+            column = jnp.zeros((PART, DK), F32)
+            for step in range(1, SIDE):
+                block = recv1[way, i, 0, step - 1]
+                total = total + block
+                before = before + jnp.where(counts(way, step, y), block, 0.0)
+                column = column + jnp.where(counts(way, step, x), recv1[way, i, 1, step - 1], 0.0)
+            row[way, i] = total
+            cols[way, i, 0] = column
+            cols[way, i, 1] = column + mine[PART:]
+            start_plane(way, 1, i)
+            local[way, i, pl.ds(0, PART)] = before
+            local[way, i, pl.ds(PART, PART)] = column
+            base_message(way, i).start()
 
     def start_third(way):
-        for j in range(2):
-            base_message(way, j).wait_recv()
-            for a in range(2):
-                wait_plane(way, 1, j, a)
-                total = base[way, j, pl.ds(64 * a, 64)]
-                for step in range(1, SIDE):
-                    block = recv2[way, j, a, step - 1]
-                    total = total + (jnp.where(counts(way, step, x), block, 0.0) if a == 0 else block)
-                pref[way, pl.ds(256 * c + j * DK + 64 * a, 64)] = total
-            pref_message(way, j).start()
+        wait_bytes(base.at[way], base_sem.at[way])
+        for i in range(PIECES):
+            wait_bytes(recv2.at[way, i], plane_sem.at[way, 1, i])
+            first = base[way, i, pl.ds(0, PART)]
+            second = base[way, i, pl.ds(PART, PART)]
+            for step in range(1, SIDE):
+                first = first + jnp.where(counts(way, step, x), recv2[way, i, 0, step - 1], 0.0)
+                second = second + recv2[way, i, 1, step - 1]
+            pref[way, piece(c, i)] = jnp.concatenate([first, second], axis=0)
+            pref_message(way, i).start()
+
+    def wait_pref(way, j):
+        wait_bytes(pref.at[way, half_head(1 - c, j)], pref_sem.at[way, j])
+
+    def leave(way):
+        wait_bytes(own.at[way], send_sem.at[way, 0])
+        wait_bytes(pref.at[way, pl.ds(0, 256)], send_sem.at[way, 1])
+        wait_bytes(base.at[way], send_sem.at[way, 2])
+        wait_bytes(recv1.at[way], send_sem.at[way, 3])
+        wait_bytes(recv2.at[way], send_sem.at[way, 4])
 
     def state(way, mine, j):
         add = c == 1 if way == 0 else c == 0
@@ -278,7 +269,7 @@
     for mine in (True, False):
         for j in range(2):
             if not mine:
-                pref_message(0, j).wait_recv()
+                wait_pref(0, j)
             at = half_head(c if mine else 1 - c, j)
             qh = q[:, at]
             total = attn[:, at] + dot(jnp.concatenate([qh, qh], axis=1), halves(state(0, mine, j), 0), NN)
@@ -303,9 +294,10 @@
     for step in (8, 7, 9, 6, 10, 5, 11, 4, 12, 3, 13, 2, 14, 1, 15):
         zmessage(step).start()
 
+    leave(0)
+    wait_bytes(zrecv, zrecv_sem)
     totals = zsend[...]
-    for step in (1, 15, 2, 14, 3, 13, 4, 12, 5, 11, 6, 10, 7, 9, 8):
-        zmessage(step).wait_recv()
+    for step in range(1, DEPTH):
         totals = totals + zrecv[step - 1]
     means = totals / FEATURES
     rms = jnp.sqrt(means[0:4] + 1e-05)
@@ -357,20 +349,11 @@
             if mine:
                 last_products(at, state(1, mine, j), k, v, dk_part, dv_part, dk, dv)
             else:
-                pref_message(1, j).wait_recv()
+                wait_pref(1, j)
                 later[pl.ds(j * DK, DK)] = state(1, mine, j)
 
-    for way in range(2):
-        for j in range(3):
-            sib_message(way, j).wait_send()
-        for j in range(2):
-            pref_message(way, j).wait_send()
-            base_message(way, j).wait_send()
-            for phase in range(2):
-                for a in range(2):
-                    leave_plane(way, phase, j, a)
-    for step in range(1, DEPTH):
-        zmessage(step).wait_send()
+    leave(1)
+    wait_bytes(zrecv, zsend_sem)
 
 
 def last_products(at, back, k, v, dk_part, dv_part, dk, dv):
@@ -430,21 +413,24 @@
             wide, wide, block, pltpu.VMEM((ROWS, DK), F32), pltpu.VMEM((ROWS, DK), F32),
             pltpu.VMEM((2, width, DK), F32),
             pltpu.VMEM((2, 2, 256, DK), F32),
-            pltpu.VMEM((2, 2, 2, 64, DK), F32),
-            pltpu.VMEM((2, 2, 2, 3, 64, DK), F32),
-            pltpu.VMEM((2, 2, 64, DK), F32),
-            pltpu.VMEM((2, 2, 2, 64, DK), F32),
-            pltpu.VMEM((2, 2, DK, DK), F32),
-            pltpu.VMEM((2, 2, DK, DK), F32),
-            pltpu.VMEM((2, 2, 2, 3, 64, DK), F32),
+            pltpu.VMEM((2, PIECES, 2, PART, DK), F32),
+            pltpu.VMEM((2, PIECES, 2, 3, PART, DK), F32),
+            pltpu.VMEM((2, PIECES, PART, DK), F32),
+            pltpu.VMEM((2, PIECES, 2, PART, DK), F32),
+            pltpu.VMEM((2, PIECES, PIECE, DK), F32),
+            pltpu.VMEM((2, PIECES, PIECE, DK), F32),
+            pltpu.VMEM((2, PIECES, 2, 3, PART, DK), F32),
             pltpu.VMEM((2, width, DK), F32),
             pltpu.VMEM((8, DK), F32),
             pltpu.VMEM((DEPTH - 1, 8, DK), F32),
             pltpu.SemaphoreType.DMA((7,)),
-            pltpu.SemaphoreType.DMA((2, 31)),
-            pltpu.SemaphoreType.DMA((2, 31)),
-            pltpu.SemaphoreType.DMA((DEPTH - 1,)),
-            pltpu.SemaphoreType.DMA((DEPTH - 1,)),
+            pltpu.SemaphoreType.DMA((2, 5)),
+            pltpu.SemaphoreType.DMA((2, 3)),
+            pltpu.SemaphoreType.DMA((2, 2)),
+            pltpu.SemaphoreType.DMA((2,)),
+            pltpu.SemaphoreType.DMA((2, 2, PIECES)),
+            pltpu.SemaphoreType.DMA,
+            pltpu.SemaphoreType.DMA,
             pltpu.SemaphoreType.REGULAR((3,)),
         ],
         compiler_params=pltpu.CompilerParams(

time: 50.7 us -> 47.8 us (0.943)
  Pallas kernels: 50 us -> 47 us
    pallas_call x1, Pallas kernels: 48.4 us -> 45.5 us  [shards(): pl.pallas_call(body, out_shape=[block, block, block, block, wide, wide, s...]
where the time goes in v5:
time: 47.8 us; the launch traced here: 47.7 us
  Pallas kernels  47 us (98%)
  between operations  0.64 us (1%)
    pallas_call x1, Pallas kernels, shards(): pl.pallas_call(body, out_shape=[block, block, block, block, wide, wide, s...  45.5 us
    pallas_call x1, Pallas kernels, shards(): pl.pallas_call(finish, out_shape=[jax.ShapeDtypeStruct((ROWS, width), BF1...  1.56 us

profile of v5, /device:TPU:1, one launch (start us, length us, event | category | flops | bytes accessed | tf_op | source)
XLA Modules:
  0.0 47.7 jit_solution(12468942661823461993)
XLA Ops:
  0.6 45.5 %attention.1 = (bf16[512,512]{1,0:T(8,128)(2,1)S(1)}, bf16[512,512]{1,0:T(8,128)(2,1)S(1)}, bf16[512,512]{1,0:T(8,128)(2,1)S(1)}, bf16[512,512]{1,0:T(8,128)(2,1...) custom-call(bf16[512,512]{1,0:T(8,128)(2,1)} %q_hbm.1, ...), custom_call_target="tpu_custom_call" | custom-call | tf_op jit(solution)/shard_map/attention/pallas_call | solution.py:404
  46.1 1.6 %finish.1 = (bf16[512,512]{1,0:T(8,128)(2,1)}, bf16[512,512]{1,0:T(8,128)(2,1)}, bf16[512,512]{1,0:T(8,128)(2,1)}, bf16[512,512]{1,0:T(8,128)(2,1)}) custom-call(bf16[512,512]{1,0:T(8,128)(2,1)S(1)} %get-tuple-element.13.normed, bf16[512,512]{1,0:T(8,128)(2,1)S(1)} %get-tuple-element.14.dq, bf16[512,512]{1,0:T(8,128)(2,1)S(1)} %get-tuple-element.15.dk_mine, ...), custom_call_target="tpu_custom_call" | custom-call | tf_op jit(solution)/shard_map/finish/pallas_call | solution.py:441

commit v6 on v5

--- a/solution.py
+++ b/solution.py
@@ -44,9 +44,9 @@
     normed, dq, dk, dv, dk_part, dv_part, later, k, v,
     q, d, gain,
     qt, scores_t, attn, g, e, inverses, weights,
-    own, sib, chip, recv1, row, cols, local, base, recv2, pref,
+    own, sib, chip, recv1, row, cols, local, recv2, pref,
     zsend, zrecv,
-    load_sem, send_sem, sib_sem, pref_sem, base_sem, plane_sem, zsend_sem, zrecv_sem, near_sem,
+    load_sem, send_sem, sib_sem, pref_sem, plane_sem, zsend_sem, zrecv_sem, near_sem, plane_near_sem,
 ):
     s = lax.axis_index("seq")
     z = lax.axis_index("head")
@@ -54,10 +54,10 @@
     sibling = (s + 1 - 2 * c, z)
 
     def along_y(step):
-        return (x * 8 + ((y + step) % SIDE) * 2 + 1 - c, z)
+        return (x * 8 + ((y + step) % SIDE) * 2 + c, z)
 
     def along_x(step):
-        return (((x + step) % SIDE) * 8 + y * 2 + 1 - c, z)
+        return (((x + step) % SIDE) * 8 + y * 2 + c, z)
 
     def along_z(step):
         return (s, (z + step) % DEPTH)
@@ -77,14 +77,13 @@
             )
         )
     ]
+    barrier = pltpu.get_barrier_semaphore()
+    partners = [sibling, along_z(1), along_z(DEPTH - 1)]
+    partners += [along_y(1), along_y(SIDE - 1), along_x(1), along_x(SIDE - 1)]
+    for partner in partners:
+        pl.semaphore_signal(barrier, inc=1, device_id=partner, device_id_type=MESH)
     for load in loads[:4]:
         load.start()
-
-    barrier = pltpu.get_barrier_semaphore()
-    partners = [sibling, along_z(1), along_z(DEPTH - 1)]
-    partners += [along_y(i) for i in range(1, SIDE)] + [along_x(i) for i in range(1, SIDE)]
-    for partner in partners:
-        pl.semaphore_signal(barrier, inc=1, device_id=partner, device_id_type=MESH)
 
     def tell(turn):
         for step in (2**turn, DEPTH - 2**turn):
@@ -92,6 +91,10 @@
 
     def hear(turn):
         pl.semaphore_wait(near_sem.at[turn], 2)
+
+    def tell_plane():
+        for device in (along_y(SIDE - 1), along_x(SIDE - 1)):
+            pl.semaphore_signal(plane_near_sem, inc=1, device_id=device, device_id_type=MESH)
 
     def half_head(half, j):
         return pl.ds(pl.multiple_of((2 * half + j) * DK, DK), DK)
@@ -113,12 +116,9 @@
     def piece(half, i):
         return pl.ds(pl.multiple_of(256 * half + PIECE * i, PIECE), PIECE)
 
-    def pref_message(way, i):
-        send, recv = send_sem.at[way, 1], pref_sem.at[way, i // (PIECES // 2)]
-        return message(send, recv, pref.at[way, piece(c, i)], pref.at[way, piece(c, i)], sibling)
-
-    def base_message(way, i):
-        return message(send_sem.at[way, 2], base_sem.at[way], local.at[way, i], base.at[way, i], sibling)
+    def pref_message(way, j):
+        at = half_head(c, j)
+        return message(send_sem.at[way, 1], pref_sem.at[way, j], pref.at[way, at], pref.at[way, at], sibling)
 
     def plane_message(way, phase, i, a, step):
         device = along_y(step) if phase == a else along_x(step)
@@ -130,7 +130,7 @@
             wrapped = (y + step) // SIDE
             pick = 1 - wrapped if way == 0 else wrapped
             src, dst = cols.at[way, i, pick], recv2.at[way, i, a, step - 1]
-        return message(send_sem.at[way, 3 + phase], plane_sem.at[way, phase, i], src, dst, device)
+        return message(send_sem.at[way, 2 + phase], plane_sem.at[way, phase, i], src, dst, device)
 
     def zmessage(step):
         return message(zsend_sem, zrecv_sem, zsend, zrecv.at[step - 1], along_z(step))
@@ -153,11 +153,9 @@
             start_plane(way, 0, i)
 
     def start_second(way):
-        sib_message(way, 2).wait_recv()
         for i in range(PIECES):
             wait_bytes(recv1.at[way, i], plane_sem.at[way, 0, i])
-            mine = own[way, piece(1 - c, i)] + sib[way, 1, pl.ds(PIECE * i, PIECE)]
-            total, before = mine[:PART], jnp.zeros((PART, DK), F32)
+            total, before = chip[way, i, 0], jnp.zeros((PART, DK), F32)
             column = jnp.zeros((PART, DK), F32)
             for step in range(1, SIDE):
                 block = recv1[way, i, 0, step - 1]
@@ -166,23 +164,23 @@
                 column = column + jnp.where(counts(way, step, x), recv1[way, i, 1, step - 1], 0.0)
             row[way, i] = total
             cols[way, i, 0] = column
-            cols[way, i, 1] = column + mine[PART:]
+            cols[way, i, 1] = column + chip[way, i, 1]
             start_plane(way, 1, i)
             local[way, i, pl.ds(0, PART)] = before
             local[way, i, pl.ds(PART, PART)] = column
-            base_message(way, i).start()
 
     def start_third(way):
-        wait_bytes(base.at[way], base_sem.at[way])
+        sib_message(way, 2).wait_recv()
         for i in range(PIECES):
             wait_bytes(recv2.at[way, i], plane_sem.at[way, 1, i])
-            first = base[way, i, pl.ds(0, PART)]
-            second = base[way, i, pl.ds(PART, PART)]
+            first = local[way, i, pl.ds(0, PART)]
+            second = local[way, i, pl.ds(PART, PART)]
             for step in range(1, SIDE):
                 first = first + jnp.where(counts(way, step, x), recv2[way, i, 0, step - 1], 0.0)
                 second = second + recv2[way, i, 1, step - 1]
             pref[way, piece(c, i)] = jnp.concatenate([first, second], axis=0)
-            pref_message(way, i).start()
+            if (i + 1) % (PIECES // 2) == 0:
+                pref_message(way, i // (PIECES // 2)).start()
 
     def wait_pref(way, j):
         wait_bytes(pref.at[way, half_head(1 - c, j)], pref_sem.at[way, j])
@@ -190,9 +188,8 @@
     def leave(way):
         wait_bytes(own.at[way], send_sem.at[way, 0])
         wait_bytes(pref.at[way, pl.ds(0, 256)], send_sem.at[way, 1])
-        wait_bytes(base.at[way], send_sem.at[way, 2])
-        wait_bytes(recv1.at[way], send_sem.at[way, 3])
-        wait_bytes(recv2.at[way], send_sem.at[way, 4])
+        wait_bytes(recv1.at[way], send_sem.at[way, 2])
+        wait_bytes(recv2.at[way], send_sem.at[way, 3])
 
     def state(way, mine, j):
         add = c == 1 if way == 0 else c == 0
@@ -223,6 +220,7 @@
         at = half_head(1 - c, j)
         own[0, at] = dot(k[:, at], v[:, at], TN)
     pl.semaphore_wait(barrier, len(partners))
+    tell_plane()
     tell(0)
     for j in range(2):
         sib_message(0, j).start()
@@ -232,9 +230,10 @@
         at = half_head(c, j)
         own[0, at] = dot(k[:, at], v[:, at], TN)
     sib_message(0, 2).start()
+    pl.semaphore_wait(plane_near_sem, 2)
+    start_first(0)
     for load in loads[4:]:
         load.wait()
-    start_first(0)
 
     def inner(h, carry):
         at = pl.ds(pl.multiple_of(h * DK, DK), DK)
@@ -418,20 +417,19 @@
             pltpu.VMEM((2, PIECES, PART, DK), F32),
             pltpu.VMEM((2, PIECES, 2, PART, DK), F32),
             pltpu.VMEM((2, PIECES, PIECE, DK), F32),
-            pltpu.VMEM((2, PIECES, PIECE, DK), F32),
             pltpu.VMEM((2, PIECES, 2, 3, PART, DK), F32),
             pltpu.VMEM((2, width, DK), F32),
             pltpu.VMEM((8, DK), F32),
             pltpu.VMEM((DEPTH - 1, 8, DK), F32),
             pltpu.SemaphoreType.DMA((7,)),
-            pltpu.SemaphoreType.DMA((2, 5)),
+            pltpu.SemaphoreType.DMA((2, 4)),
             pltpu.SemaphoreType.DMA((2, 3)),
             pltpu.SemaphoreType.DMA((2, 2)),
-            pltpu.SemaphoreType.DMA((2,)),
             pltpu.SemaphoreType.DMA((2, 2, PIECES)),
             pltpu.SemaphoreType.DMA,
             pltpu.SemaphoreType.DMA,
             pltpu.SemaphoreType.REGULAR((3,)),
+            pltpu.SemaphoreType.REGULAR,
         ],
         compiler_params=pltpu.CompilerParams(
             collective_id=0, has_side_effects=True, vmem_limit_bytes=32 * 1024 * 1024

time: 47.8 us -> 47.8 us (level)
  no operation moved by 1% of the time
where the time goes in v6:
time: 47.8 us; the launch traced here: 47.6 us
  Pallas kernels  47 us (98%)
  between operations  0.64 us (1%)
    pallas_call x1, Pallas kernels, shards(): pl.pallas_call(body, out_shape=[block, block, block, block, wide, wide, s...  45.4 us
    pallas_call x1, Pallas kernels, shards(): pl.pallas_call(finish, out_shape=[jax.ShapeDtypeStruct((ROWS, width), BF1...  1.57 us

profile of v6, /device:TPU:1, one launch (start us, length us, event | category | flops | bytes accessed | tf_op | source)
XLA Modules:
  0.0 47.6 jit_solution(9165667597298655979)
XLA Ops:
  0.6 45.4 %attention.1 = (bf16[512,512]{1,0:T(8,128)(2,1)S(1)}, bf16[512,512]{1,0:T(8,128)(2,1)S(1)}, bf16[512,512]{1,0:T(8,128)(2,1)S(1)}, bf16[512,512]{1,0:T(8,128)(2,1...) custom-call(bf16[512,512]{1,0:T(8,128)(2,1)} %q_hbm.1, ...), custom_call_target="tpu_custom_call" | custom-call | tf_op jit(solution)/shard_map/attention/pallas_call | solution.py:403
  46.1 1.6 %finish.1 = (bf16[512,512]{1,0:T(8,128)(2,1)}, bf16[512,512]{1,0:T(8,128)(2,1)}, bf16[512,512]{1,0:T(8,128)(2,1)}, bf16[512,512]{1,0:T(8,128)(2,1)}) custom-call(bf16[512,512]{1,0:T(8,128)(2,1)S(1)} %get-tuple-element.13.normed, bf16[512,512]{1,0:T(8,128)(2,1)S(1)} %get-tuple-element.14.dq, bf16[512,512]{1,0:T(8,128)(2,1)S(1)} %get-tuple-element.15.dk_mine, ...), custom_call_target="tpu_custom_call" | custom-call | tf_op jit(solution)/shard_map/finish/pallas_call | solution.py:439

commit v7 on v6

--- a/solution.py
+++ b/solution.py
@@ -40,9 +40,9 @@
 
 
 def body(
-    q_hbm, k_hbm, v_hbm, gain_hbm, d_hbm,
+    q_hbm, k_hbm, v_hbm, gain, d_hbm,
     normed, dq, dk, dv, dk_part, dv_part, later, k, v,
-    q, d, gain,
+    q, d,
     qt, scores_t, attn, g, e, inverses, weights,
     own, sib, chip, recv1, row, cols, local, recv2, pref,
     zsend, zrecv,
@@ -73,7 +73,6 @@
                 (v_hbm.at[:, here], v.at[:, here]),
                 (q_hbm, q),
                 (d_hbm, d),
-                (gain_hbm, gain),
             )
         )
     ]
@@ -158,14 +157,14 @@
             total, before = chip[way, i, 0], jnp.zeros((PART, DK), F32)
             column = jnp.zeros((PART, DK), F32)
             for step in range(1, SIDE):
-                block = recv1[way, i, 0, step - 1]
-                total = total + block
-                before = before + jnp.where(counts(way, step, y), block, 0.0)
+                total = total + recv1[way, i, 0, step - 1]
                 column = column + jnp.where(counts(way, step, x), recv1[way, i, 1, step - 1], 0.0)
             row[way, i] = total
             cols[way, i, 0] = column
             cols[way, i, 1] = column + chip[way, i, 1]
             start_plane(way, 1, i)
+            for step in range(1, SIDE):
+                before = before + jnp.where(counts(way, step, y), recv1[way, i, 0, step - 1], 0.0)
             local[way, i, pl.ds(0, PART)] = before
             local[way, i, pl.ds(PART, PART)] = column
 
@@ -258,7 +257,7 @@
 
     lax.fori_loop(0, HEADS_HERE, prepare, 0)
     for h in range(HEADS_HERE):
-        g[:, head(h)] = d[:, head(h)].astype(F32) * gain[h : h + 1, :].astype(F32)
+        g[:, head(h)] = d[:, head(h)].astype(F32) * gain[h : h + 1, :]
     hear(1)
     tell(2)
     start_third(0)
@@ -317,7 +316,7 @@
     sib_message(1, 2).start()
     start_first(1)
     for h in range(HEADS_HERE):
-        normed[:, head(h)] = (attn[:, head(h)] * inverses[...] * gain[h : h + 1, :].astype(F32)).astype(BF16)
+        normed[:, head(h)] = (attn[:, head(h)] * inverses[...] * gain[h : h + 1, :]).astype(BF16)
 
     def outer(h, carry):
         at = pl.ds(pl.multiple_of(h * DK, DK), DK)
@@ -399,14 +398,17 @@
     states = pltpu.VMEM((256, DK), F32)
     in_hbm = pl.BlockSpec(memory_space=pltpu.HBM)
     in_vmem = pl.BlockSpec(memory_space=pltpu.VMEM)
-    arguments = (queries, keys, values, gain.reshape(HEADS_HERE, DK), d_out)
+    gain = gain.astype(F32).reshape(HEADS_HERE, DK)
+    queries, keys, values, d_out = (
+        pltpu.with_memory_space_constraint(array, pltpu.HBM) for array in (queries, keys, values, d_out)
+    )
     partial = pl.pallas_call(
         body,
         out_shape=[block, block, block, block, wide, wide, states, block, block],
-        in_specs=[in_hbm] * 5,
+        in_specs=[in_hbm, in_hbm, in_hbm, in_vmem, in_hbm],
         out_specs=[in_vmem] * 9,
         scratch_shapes=[
-            block, block, pltpu.VMEM((HEADS_HERE, DK), BF16),
+            block, block,
             pltpu.VMEM((width, ROWS), BF16),
             pltpu.VMEM((HEADS_HERE, ROWS, ROWS), BF16),
             wide, wide, block, pltpu.VMEM((ROWS, DK), F32), pltpu.VMEM((ROWS, DK), F32),
@@ -421,7 +423,7 @@
             pltpu.VMEM((2, width, DK), F32),
             pltpu.VMEM((8, DK), F32),
             pltpu.VMEM((DEPTH - 1, 8, DK), F32),
-            pltpu.SemaphoreType.DMA((7,)),
+            pltpu.SemaphoreType.DMA((6,)),
             pltpu.SemaphoreType.DMA((2, 4)),
             pltpu.SemaphoreType.DMA((2, 3)),
             pltpu.SemaphoreType.DMA((2, 2)),
@@ -435,7 +437,7 @@
             collective_id=0, has_side_effects=True, vmem_limit_bytes=32 * 1024 * 1024
         ),
         name="attention",
-    )(*[pltpu.with_memory_space_constraint(array, pltpu.HBM) for array in arguments])
+    )(queries, keys, values, gain, d_out)
     return pl.pallas_call(
         finish,
         out_shape=[jax.ShapeDtypeStruct((ROWS, width), BF16)] * 4,

time: 47.8 us -> 48.4 us (1.013)
  other arithmetic: 0 us -> 0.68 us
    reshape x0 -> x1, other arithmetic: none -> 0.68 us  [shards(): gain = gain.astype(F32).reshape(HEADS_HERE, DK)]
where the time goes in v7:
time: 48.4 us; the launch traced here: 48.3 us
  Pallas kernels  47 us (97%)
  other arithmetic  0.68 us (1%)
  between operations  0.64 us (1%)
    pallas_call x1, Pallas kernels, shards(): pl.pallas_call(body, out_shape=[block, block, block, block, wide, wide, s...  45.4 us
    pallas_call x1, Pallas kernels, shards(): pl.pallas_call(finish, out_shape=[jax.ShapeDtypeStruct((ROWS, width), BF1...  1.57 us

profile of v7, /device:TPU:1, one launch (start us, length us, event | category | flops | bytes accessed | tf_op | source)
XLA Modules:
  0.0 48.3 jit_solution(3359963688959305090)
XLA Ops:
  0.6 0.7 %bitcast_convert_fusion.gain = f32[4,128]{1,0:T(4,128)S(1)} fusion(bf16[512]{0:T(512)(128)(2,1)} %param.8), kind=kLoop, calls=%fused_computation | loop fusion | flops 512 | bytes 3072 | tf_op jit(solution)/shard_map/reshape | solution.py:401
  1.3 45.4 %attention.1 = (bf16[512,512]{1,0:T(8,128)(2,1)S(1)}, bf16[512,512]{1,0:T(8,128)(2,1)S(1)}, bf16[512,512]{1,0:T(8,128)(2,1)S(1)}, bf16[512,512]{1,0:T(8,128)(2,1...) custom-call(bf16[512,512]{1,0:T(8,128)(2,1)} %q_hbm.1, ...), custom_call_target="tpu_custom_call" | custom-call | tf_op jit(solution)/shard_map/attention/pallas_call | solution.py:405
  46.7 1.6 %finish.1 = (bf16[512,512]{1,0:T(8,128)(2,1)}, bf16[512,512]{1,0:T(8,128)(2,1)}, bf16[512,512]{1,0:T(8,128)(2,1)}, bf16[512,512]{1,0:T(8,128)(2,1)}) custom-call(bf16[512,512]{1,0:T(8,128)(2,1)S(1)} %get-tuple-element.13.normed, bf16[512,512]{1,0:T(8,128)(2,1)S(1)} %get-tuple-element.14.dq, bf16[512,512]{1,0:T(8,128)(2,1)S(1)} %get-tuple-element.15.dk_mine, ...), custom_call_target="tpu_custom_call" | custom-call | tf_op jit(solution)/shard_map/finish/pallas_call | solution.py:441

commit v8 on v6

--- a/solution.py
+++ b/solution.py
@@ -158,14 +158,14 @@
             total, before = chip[way, i, 0], jnp.zeros((PART, DK), F32)
             column = jnp.zeros((PART, DK), F32)
             for step in range(1, SIDE):
-                block = recv1[way, i, 0, step - 1]
-                total = total + block
-                before = before + jnp.where(counts(way, step, y), block, 0.0)
+                total = total + recv1[way, i, 0, step - 1]
                 column = column + jnp.where(counts(way, step, x), recv1[way, i, 1, step - 1], 0.0)
             row[way, i] = total
             cols[way, i, 0] = column
             cols[way, i, 1] = column + chip[way, i, 1]
             start_plane(way, 1, i)
+            for step in range(1, SIDE):
+                before = before + jnp.where(counts(way, step, y), recv1[way, i, 0, step - 1], 0.0)
             local[way, i, pl.ds(0, PART)] = before
             local[way, i, pl.ds(PART, PART)] = column
 

time: 47.8 us -> 47.8 us (level)
  no operation moved by 1% of the time
where the time goes in v8:
time: 47.8 us; the launch traced here: 47.6 us
  Pallas kernels  47 us (98%)
  between operations  0.64 us (1%)
    pallas_call x1, Pallas kernels, shards(): pl.pallas_call(body, out_shape=[block, block, block, block, wide, wide, s...  45.4 us
    pallas_call x1, Pallas kernels, shards(): pl.pallas_call(finish, out_shape=[jax.ShapeDtypeStruct((ROWS, width), BF1...  1.57 us

profile of v8, /device:TPU:1, one launch (start us, length us, event | category | flops | bytes accessed | tf_op | source)
XLA Modules:
  0.0 47.6 jit_solution(6257742695346720254)
XLA Ops:
  0.6 45.4 %attention.1 = (bf16[512,512]{1,0:T(8,128)(2,1)S(1)}, bf16[512,512]{1,0:T(8,128)(2,1)S(1)}, bf16[512,512]{1,0:T(8,128)(2,1)S(1)}, bf16[512,512]{1,0:T(8,128)(2,1...) custom-call(bf16[512,512]{1,0:T(8,128)(2,1)} %q_hbm.1, ...), custom_call_target="tpu_custom_call" | custom-call | tf_op jit(solution)/shard_map/attention/pallas_call | solution.py:403
  46.1 1.6 %finish.1 = (bf16[512,512]{1,0:T(8,128)(2,1)}, bf16[512,512]{1,0:T(8,128)(2,1)}, bf16[512,512]{1,0:T(8,128)(2,1)}, bf16[512,512]{1,0:T(8,128)(2,1)}) custom-call(bf16[512,512]{1,0:T(8,128)(2,1)S(1)} %get-tuple-element.13.normed, bf16[512,512]{1,0:T(8,128)(2,1)S(1)} %get-tuple-element.14.dq, bf16[512,512]{1,0:T(8,128)(2,1)S(1)} %get-tuple-element.15.dk_mine, ...), custom_call_target="tpu_custom_call" | custom-call | tf_op jit(solution)/shard_map/finish/pallas_call | solution.py:439
